TPU v7x, 256 devices: a whole 4x4x8 slice. The times are simulated.
256 devices in a mesh: ctx: 4 (over y), cache: 32 (over z, x_lo, core), head: 2 (over x_hi).
Axes of the slice: x: 4 (x_hi: 2, x_lo: 2; x = x_hi * 2 + x_lo), y: 4, z: 8, core: 2. Of those that a mesh axis runs over, the one named last changes fastest.
Arguments:
- queries: bfloat16 [32, 768, 4096], P('cache', 'ctx', 'head'), may hold values from -8 to 8
- fresh_kv: bfloat16 [32, 768, 4, 256], P('cache', 'ctx', 'head'), may hold values from -5 to 5
- kv_store: bfloat16 [2048, 32, 4, 256], P('cache', None, 'head'), may hold values from -6 to 6
- page_owner: int32 [32, 128, 1], P('cache'), may hold values from 0 to 31; in each aligned block of 32 rows (0 to 31, 32 to 63, ..., all dimensions but the last counted through in order) at most 2 rows name the same one
- page_slot: int32 [32, 128], P('cache'), may hold values from 0 to 63
- rec_index: int32 [32, 768], P('cache'), may hold values from 0 to 1023, as said below
Outputs:
- attended: bfloat16 [32, 768, 4096], P('cache', 'ctx', 'head')
Inputs may be any that keep to these rules, and one draw needn't show every extreme that they name: `page_owner`: no shard holds more than 2 of the pages of one block (aligned blocks of 32 rows). `rec_index`: each block of 192 entries holds distinct positions in ascending order; the last is always 1024 - 1.
All inputs are finite; a program needn't handle non-finite values.
Results may differ from a plain program's by a relative error of at most 0.0039.
Values may be sent and summed in bfloat16 or wider, within the bound.
A program may use at most 64 MiB of HBM per device.

v0:
```python
import jax
import jax.numpy as jnp
from jax import lax
from jax.sharding import PartitionSpec as P

NEGATIVE = -1e30


def attend_rows(state, queries, query_pos, key_rows, first_pos):
    row_max, row_sum, weighted = state
    head_dim = queries.shape[-1]
    scores = jnp.einsum(
        "rkgh,lkh->kgrl", queries, key_rows[:, :, :head_dim], preferred_element_type=jnp.float32
    ) * head_dim ** (-0.5)
    key_pos = first_pos + lax.iota(jnp.int32, key_rows.shape[0])
    visible = key_pos[None, :] <= query_pos[:, None]
    masked = jnp.where(visible, scores, NEGATIVE)
    new_max = jnp.maximum(row_max, jnp.max(masked, axis=-1))
    weights = jnp.where(visible, jnp.exp(masked - new_max[..., None]), 0.0)
    factor = jnp.exp(row_max - new_max)
    row_sum = row_sum * factor + jnp.sum(weights, axis=-1)
    weighted = weighted * factor[..., None] + jnp.einsum(
        "kgrl,lkh->kgrh",
        weights.astype(jnp.bfloat16),
        key_rows[:, :, head_dim:],
        preferred_element_type=jnp.float32,
    )
    return (new_max, row_sum, weighted)


def fold_group(state, group_rows, key_rows, first_pos):
    queries, query_pos, last_pos = group_rows
    length = key_rows.shape[0]
    stride = min(length, 1024)
    for offset in range(0, length, stride):
        portion = key_rows[offset : offset + stride]
        portion_pos = first_pos + offset

        def advance(current, portion=portion, portion_pos=portion_pos):
            return attend_rows(current, queries, query_pos, portion, portion_pos)

        def remain(current):
            return current

        state = lax.cond(portion_pos <= last_pos, advance, remain, state)
    return state


def empty_state(queries):
    rows, kv_heads, group_size, head_dim = queries.shape
    return (
        jnp.full((kv_heads, group_size, rows), NEGATIVE, jnp.float32),
        jnp.zeros((kv_heads, group_size, rows), jnp.float32),
        jnp.zeros((kv_heads, group_size, rows, head_dim), jnp.float32),
    )


def finish_rows(state):
    row_max, row_sum, weighted = state
    mixed = weighted / row_sum[..., None]
    return mixed.transpose(2, 0, 1, 3).reshape(mixed.shape[2], -1).astype(jnp.bfloat16)


def plan_requests(owners, slot_ids, wanted, capacity, cache_count):
    one_hot = (owners[:, None] == lax.iota(jnp.int32, cache_count)[None, :]) & wanted[:, None]
    counts = jnp.cumsum(one_hot.astype(jnp.int32), axis=0)
    ranking = jnp.sum(jnp.where(one_hot, counts, 0), axis=1) - 1
    target_slot = jnp.where(wanted, owners * capacity + ranking, cache_count * capacity)
    requests = jnp.full((cache_count * capacity + 1,), -1, jnp.int32).at[target_slot].set(slot_ids)
    return (requests[:-1].reshape(cache_count, capacity), target_slot)


def pick_pages(received, target_slot):
    flat_pages = received.reshape((-1,) + received.shape[2:])
    return jnp.take(flat_pages, jnp.minimum(target_slot, flat_pages.shape[0] - 1), axis=0)


def shards(queries, fresh_kv, kv_store, page_owner, page_slot, rec_index):
    ctx_count = lax.axis_size("ctx")
    cache_count = lax.axis_size("cache")
    block_index = lax.axis_index("ctx")
    rec_rows = queries.shape[1]
    kv_heads = fresh_kv.shape[2]
    head_dim = fresh_kv.shape[3] // 2
    group_size = queries.shape[2] // head_dim // kv_heads
    page_len = kv_store.shape[1]
    pages_prompt = page_owner.shape[1]
    pages_dev = pages_prompt // ctx_count
    tok_dev = pages_dev * page_len
    capacity = 2 * ((pages_dev + cache_count - 1) // cache_count)
    owners = page_owner[0, :, 0]
    slot_ids = page_slot[0]
    rec_all = rec_index[0]
    own_queries = queries[0].reshape(rec_rows, kv_heads, group_size, head_dim)
    own_rec = lax.dynamic_slice_in_dim(rec_all, block_index * rec_rows, rec_rows)
    own_pos = block_index * tok_dev + own_rec
    groups = [(own_queries, own_pos, jnp.max(own_pos))]

    def fold_all(states, key_rows, first_pos):
        return tuple(
            (
                fold_group(state_one, group_rows, key_rows, first_pos)
                for state_one, group_rows in zip(states, groups)
            )
        )

    initial = tuple((empty_state(group_rows[0]) for group_rows in groups))
    own_owners = lax.dynamic_slice_in_dim(owners, block_index * pages_dev, pages_dev)
    own_slots = lax.dynamic_slice_in_dim(slot_ids, block_index * pages_dev, pages_dev)
    wanted = jnp.ones((pages_dev,), bool)
    requests, target_slot = plan_requests(own_owners, own_slots, wanted, capacity, cache_count)
    found_pages = jnp.take(
        kv_store,
        jnp.maximum(lax.all_to_all(requests, "cache", split_axis=0, concat_axis=0, tiled=True), 0),
        axis=0,
    )
    received = lax.all_to_all(found_pages, "cache", split_axis=0, concat_axis=0, tiled=True)
    cached = pick_pages(received, target_slot).reshape(tok_dev, kv_heads, 2 * head_dim)
    merged = cached.at[own_rec].set(fresh_kv[0])
    states = fold_all(initial, lax.all_gather(merged, "ctx", axis=0, tiled=True), jnp.int32(0))
    results = [finish_rows(state_one) for state_one in states]
    complete = results[0]
    return complete[None]


def solution(mesh):
    in_specs = (
        P("cache", "ctx", "head"),
        P("cache", "ctx", "head", None),
        P("cache", None, "head", None),
        P("cache", None, None),
        P("cache", None),
        P("cache", None),
    )
    out_specs = P("cache", "ctx", "head")
    return jax.shard_map(shards, mesh=mesh, in_specs=in_specs, out_specs=out_specs, check_vma=False)
```

profile of v0, /device:TPU:24, one launch (start us, length us, event | category | flops | bytes accessed | tf_op | source)
XLA Modules:
  0.0 234.4 jit_solution(13843291107168803009)
XLA Ops:
  6.5 0.9 fusion.61
  10.0 17.8 %all_to_all.14 = s32[32,1,2]{2,1,0:T(1,128)S(1)} all-to-all(s32[32,1,2]{2,1,0:T(1,128)S(1)} %bitcast.144), channel_id=1, replica_groups=mesh['ctx'=4,'cache'=32,'head'=2] {'cache'}, dimensions={0} | all-to-all | bytes 512 | tf_op jit(solution)/shard_map/all_to_all | solution.py:114
  28.2 6.8 %gather_fusion = bf16[64,32,2,256]{3,2,1,0:T(2,128)(2,1)} fusion(bf16[64,32,2,256]{3,2,1,0:T(2,128)(2,1)S(1)} %copy-done, s32[1024]{0:T(1024)S(1)} %pad_clamp_fusion.1), kind=kCustom, calls=%fused_computation | custom fusion | bytes 4194560 | tf_op jit(solution)/shard_map/jit(_take)/gather | solution.py:112
  35.0 3.2 %copy_select_fusion = bf16[32,2,32,2,256]{4,2,3,1,0:T(8,128)(2,1)} fusion(bf16[32,2,32,2,256]{4,3,2,1,0:T(2,128)(2,1)} %bitcast.139, pred[32,2]{1,0:T(8,128)(4,1)S(1)} %copy.39), kind=kLoop, calls=%fused_computation.80 | loop fusion | flops 1048576 | bytes 4194368 | tf_op jit(solution)/shard_map/jit(_take)/select_n | solution.py:112
  38.2 4.0 %all-to-all-start.1 = ((bf16[32,2,32,2,256]{4,2,3,1,0:T(8,128)(2,1)}), bf16[32,2,32,2,256]{4,2,3,1,0:T(8,128)(2,1)S(1)}, u32[]{:S(2)}, u32[]{:S(2)}) async-start(bf16[32,2,32,2,256]{4,2,3,1,0:T(8,128)(2,1)} %copy_select_fusion), calls=%async_computation.1 | async-start | bytes 4194304 | tf_op jit(solution)/shard_map/all_to_all | solution.py:117
  42.6 51.3 %all-to-all-done.1 = bf16[32,2,32,2,256]{4,2,3,1,0:T(8,128)(2,1)S(1)} async-done(((bf16[32,2,32,2,256]{4,2,3,1,0:T(8,128)(2,1)}), bf16[32,2,32,2,256]{4,2,3,1,0:T(8,128)(2,1)S(1)}, u32[]{:S(2)}, u32[]{:S(2)}) %all-to-all-start.1) | async-done | bytes 2097184 | tf_op jit(solution)/shard_map/all_to_all | solution.py:117
  94.6 8.2 %broadcast_select_fusion = bf16[1024,2,256]{2,1,0:T(2,128)(2,1)S(1)} fusion(pred[1024]{0:T(1024)(128)(4,1)S(1)} %broadcast_in_dim.121, bf16[1024,2,256]{2,0,1:T(8,128)(2,1)S(1)} %bitcast.141), kind=kLoop, calls=%fused_computation.81 | loop fusion | flops 524288 | bytes 2098176 | tf_op jit(solution)/shard_map/jit(_take)/select_n | solution.py:75
  102.8 6.2 %scatter_fusion = bf16[1024,2,256]{2,1,0:T(2,128)(2,1)S(1)} fusion(bf16[1024,2,256]{2,1,0:T(2,128)(2,1)S(1)} %broadcast_select_fusion, s32[192]{0:T(256)S(1)} %bitcast.149, bf16[192,2,256]{2,1,0:T(2,128)(2,1)S(1)} %bitcast.143), kind=kCustom, calls=%fused_computation.3 | custom fusion | bytes 590592 | tf_op jit(solution)/shard_map/scatter | solution.py:119
  109.1 1.0 copy-done.2
  113.4 1.3 copy.60
  114.7 40.7 %all-gather.2.cloned.1.call-done = bf16[4096,2,256]{2,1,0:T(2,128)(2,1)} async-done(((bf16[1024,2,256]{2,1,0:T(2,128)(2,1)}), bf16[4096,2,256]{2,1,0:T(2,128)(2,1)}) %all-gather.2.cloned.1.call-update) | async-done | bytes 4194320 | tf_op jit(solution)/shard_map/all_gather | solution.py:120
  155.3 2.7 %fusion.63 = (bf16[1024,2,256]{2,1,0:T(2,128)(2,1)S(1)}, bf16[1024,2,256]{2,1,0:T(2,128)(2,1)S(1)}) fusion(bf16[4096,2,256]{2,1,0:T(2,128)(2,1)} %all-gather.2.cloned.1.call-done), kind=kLoop, calls=%fused_computation.108 | loop fusion | bytes 4194304 | tf_op jit(solution)/shard_map/slice | solution.py:36
  158.0 15.1 %conditional.4 = (f32[2,8,192]{2,1,0:T(8,128)}, f32[2,8,192]{2,1,0:T(8,128)S(1)}, f32[2,8,192,128]{3,2,1,0:T(8,128)}) conditional(s32[]{:T(128)} %convert_element_type.46, () %tuple.32, (s32[192]{0:T(256)S(1)}, bf16[1024,2,256]{2,1,0:T(2,128)(2,1)S(1)}, bf16[192,2,8,128]{3,2,1,0:T(8,128)(2,1)S(1)}) %tuple.81), branch_computations={%region_5.6_spmd, %region_6.9_spmd} | conditional | flops 1652109312 | bytes 44180248 | solution.py:45
  158.5 2.6 %fusion = (f32[2,8,192]{2,1,0:T(8,128)S(1)}, f32[2,1024,192,8]{1,2,3,0:T(8,128)S(1)}) fusion(pred[192,1024]{1,0:T(8,128)(4,1)S(1)} %iota_compare_fusion, bf16[192,2,8,128]{3,2,1,0:T(8,128)(2,1)S(1)} %get-tuple-element.152, bf16[1024,2,256]{2,0,1:T(8,128)(2,1)S(1)} %copy.43), kind=kOutput, calls=%fused_computation.6 | convolution fusion | flops 814740480 | bytes 14102528 | tf_op jit(solution)/shard_map/cond/branch_1_fun/rkgh,lkh->kgrl/dot_general | solution.py:12
  161.7 5.0 %fusion.2 = f32[2,8,192]{2,1,0:T(8,128)S(1)} fusion(f32[2,1024,192,8]{1,2,3,0:T(8,128)S(1)} %get-tuple-element.184, f32[2,8,192]{2,1,0:T(8,128)} %get-tuple-element.196, pred[192,1024]{1,0:T(8,128)(4,1)S(1)} %iota_compare_fusion), kind=kLoop, calls=%fused_computation.8 | loop fusion | flops 15725568 | bytes 12804096 | tf_op jit(solution)/shard_map/cond/branch_1_fun/reduce_sum | solution.py:21
  167.4 5.7 %fusion.6 = f32[2,8,192,128]{3,2,1,0:T(8,128)} fusion(f32[2,1024,192,8]{1,2,3,0:T(8,128)S(1)} %get-tuple-element.184, f32[2,8,192]{2,1,0:T(8,128)} %get-tuple-element.196, pred[192,1024]{1,0:T(8,128)(4,1)S(1)} %iota_compare_fusion, f32[2,8,192]{2,1,0:T(8,128)S(1)} %get-tuple-element.171, bf16[1024,2,256]{2,0,1:T(8,128)(2,1)S(1)} %copy.43), kind=kOutput, calls=%fused_computation.11 | convolution fusion | flops 821428224 | bytes 14905344 | tf_op jit(solution)/shard_map/cond/branch_1_fun/kgrl,lkh->kgrh/dot_general | solution.py:22
  173.1 15.3 %conditional.5 = ((f32[2,8,192]{2,1,0:T(8,128)}, f32[2,8,192]{2,1,0:T(8,128)S(1)}, f32[2,8,192,128]{3,2,1,0:T(8,128)})) conditional(s32[]{:T(128)} %convert_element_type.45, (f32[2,8,192]{2,1,0:T(8,128)}, f32[2,8,192]{2,1,0:T(8,128)S(1)}, f32[2,8,192,128]{3,2,1,0:T(8,128)}) %conditional.4, (s32[192]{0:T(256)S(1)}, ...), branch_computations={%region_9.10_spmd, %region_10.13_spmd} | conditional | flops 1652497408 | bytes 45826848 | solution.py:45
  173.5 2.6 %fusion.15 = (f32[2,8,192]{2,1,0:T(8,128)S(1)}, f32[2,1024,192,8]{1,2,3,0:T(8,128)S(1)}) fusion(pred[192,1024]{1,0:T(8,128)(4,1)S(1)} %broadcast_compare_fusion, bf16[192,2,8,128]{3,2,1,0:T(8,128)(2,1)S(1)} %get-tuple-element.155, bf16[1024,2,256]{2,0,1:T(8,128)(2,1)S(1)} %copy.45), kind=kOutput, calls=%fused_computation.25 | convolution fusion | flops 814740480 | bytes 14102528 | tf_op jit(solution)/shard_map/cond/branch_1_fun/rkgh,lkh->kgrl/dot_general | solution.py:12
  176.8 4.3 %fusion.17 = f32[2,8,192]{2,1,0:T(8,128)S(1)} fusion(f32[2,1024,192,8]{1,2,3,0:T(8,128)S(1)} %get-tuple-element.186, f32[2,8,192]{2,1,0:T(8,128)S(1)} %max.22, pred[192,1024]{1,0:T(8,128)(4,1)S(1)} %broadcast_compare_fusion), kind=kLoop, calls=%fused_computation.27 | loop fusion | flops 15725568 | bytes 12804096 | tf_op jit(solution)/shard_map/cond/branch_1_fun/reduce_sum | solution.py:21
  182.4 6.1 %multiply_add_fusion = f32[2,8,192,128]{3,2,1,0:T(8,128)} fusion(f32[2,8,192,128]{3,2,1,0:T(8,128)} %get-tuple-element.73, f32[2,1024,192,8]{1,2,3,0:T(8,128)S(1)} %get-tuple-element.186, f32[2,8,192]{2,1,0:T(8,128)S(1)} %max.22, pred[192,1024]{1,0:T(8,128)(4,1)S(1)} %broadcast_compare_fusion, f32[2,8,192]{2,1,0:T(8,128)S(1)} %get-tuple-element.174, ...), kind=kOutput, calls=%fused_computation.30 | convolution fusion | flops 821821440 | bytes 16482304 | tf_op jit(solution)/shard_map/cond/branch_1_fun/kgrl,lkh->kgrh/dot_general | solution.py:22
  188.5 17.9 %conditional.6 = ((f32[2,8,192]{2,1,0:T(8,128)}, f32[2,8,192]{2,1,0:T(8,128)S(1)}, f32[2,8,192,128]{3,2,1,0:T(8,128)})) conditional(s32[]{:T(128)} %convert_element_type.44, (f32[2,8,192]{2,1,0:T(8,128)}, f32[2,8,192]{2,1,0:T(8,128)S(1)}, f32[2,8,192,128]{3,2,1,0:T(8,128)}) %get-tuple-element.215, (s32[192]{0:T(256)S(1)}, ...), branch_computations={%region_13.14_spmd, %region_14.17_spmd} | conditional | flops 1652497408 | bytes 52118304 | solution.py:45
  188.7 2.7 %copy.47 = bf16[4096,2,256]{2,0,1:T(8,128)(2,1)S(1)} copy(bf16[4096,2,256]{2,1,0:T(2,128)(2,1)} %get-tuple-element.160) | data formatting | bytes 8388608 | tf_op jit(solution)/shard_map
  191.4 2.6 %fusion.28 = (f32[2,8,192]{2,1,0:T(8,128)S(1)}, f32[2,1024,192,8]{1,2,3,0:T(8,128)S(1)}) fusion(pred[192,1024]{1,0:T(8,128)(4,1)S(1)} %broadcast_compare_fusion.1, bf16[192,2,8,128]{3,2,1,0:T(8,128)(2,1)S(1)} %get-tuple-element.161, bf16[4096,2,256]{2,0,1:T(8,128)(2,1)S(1)} %copy.47), kind=kOutput, calls=%fused_computation.44 | convolution fusion | flops 814740480 | bytes 14102528 | tf_op jit(solution)/shard_map/cond/branch_1_fun/rkgh,lkh->kgrl/dot_general | solution.py:12
  194.7 4.2 %fusion.30 = f32[2,8,192]{2,1,0:T(8,128)S(1)} fusion(f32[2,1024,192,8]{1,2,3,0:T(8,128)S(1)} %get-tuple-element.188, f32[2,8,192]{2,1,0:T(8,128)S(1)} %max.23, pred[192,1024]{1,0:T(8,128)(4,1)S(1)} %broadcast_compare_fusion.1), kind=kLoop, calls=%fused_computation.46 | loop fusion | flops 15725568 | bytes 12804096 | tf_op jit(solution)/shard_map/cond/branch_1_fun/reduce_sum | solution.py:21
  200.3 6.1 %multiply_add_fusion.2 = f32[2,8,192,128]{3,2,1,0:T(8,128)} fusion(f32[2,8,192,128]{3,2,1,0:T(8,128)} %get-tuple-element.79, f32[2,1024,192,8]{1,2,3,0:T(8,128)S(1)} %get-tuple-element.188, f32[2,8,192]{2,1,0:T(8,128)S(1)} %max.23, pred[192,1024]{1,0:T(8,128)(4,1)S(1)} %broadcast_compare_fusion.1, f32[2,8,192]{2,1,0:T(8,128)S(1)} %get-tuple-element.176, ...), kind=kOutput, calls=%fused_computation.49 | convolution fusion | flops 821821440 | bytes 16482304 | tf_op jit(solution)/shard_map/cond/branch_1_fun/kgrl,lkh->kgrh/dot_general | solution.py:22
  206.4 17.4 %conditional.7 = ((f32[2,8,192]{2,1,0:T(8,128)S(1)}, f32[2,8,192,128]{3,2,1,0:T(8,128)})) conditional(s32[]{:T(128)} %convert_element_type.43, (f32[2,8,192]{2,1,0:T(8,128)S(1)}, f32[2,8,192,128]{3,2,1,0:T(8,128)}) %tuple.36, (s32[192]{0:T(256)S(1)}, bf16[4096,2,256]{2,1,0:T(2,128)(2,1)}, bf16[192,2,8,128]{3,2,1,0:T(8,128)(2,1)S(1)}, ...), branch_computations={%region_17.18_spmd, %region_18.21_spmd} | conditional | flops 1652497408 | bytes 52093720 | solution.py:45
  206.6 2.7 %copy.49 = bf16[4096,2,256]{2,0,1:T(8,128)(2,1)S(1)} copy(bf16[4096,2,256]{2,1,0:T(2,128)(2,1)} %get-tuple-element.166) | data formatting | bytes 8388608 | tf_op jit(solution)/shard_map
  209.3 2.6 %fusion.41 = (f32[2,8,192]{2,1,0:T(8,128)S(1)}, f32[2,1024,192,8]{1,2,3,0:T(8,128)S(1)}) fusion(pred[192,1024]{1,0:T(8,128)(4,1)S(1)} %broadcast_compare_fusion.2, bf16[192,2,8,128]{3,2,1,0:T(8,128)(2,1)S(1)} %get-tuple-element.167, bf16[4096,2,256]{2,0,1:T(8,128)(2,1)S(1)} %copy.49), kind=kOutput, calls=%fused_computation.63 | convolution fusion | flops 814740480 | bytes 14102528 | tf_op jit(solution)/shard_map/cond/branch_1_fun/rkgh,lkh->kgrl/dot_general | solution.py:12
  212.6 4.2 %fusion.43 = f32[2,8,192]{2,1,0:T(8,128)S(1)} fusion(f32[2,1024,192,8]{1,2,3,0:T(8,128)S(1)} %get-tuple-element.190, f32[2,8,192]{2,1,0:T(8,128)S(1)} %max.24, pred[192,1024]{1,0:T(8,128)(4,1)S(1)} %broadcast_compare_fusion.2), kind=kLoop, calls=%fused_computation.65 | loop fusion | flops 15725568 | bytes 12804096 | tf_op jit(solution)/shard_map/cond/branch_1_fun/reduce_sum | solution.py:21
  217.6 6.2 %multiply_add_fusion.4 = f32[2,8,192,128]{3,2,1,0:T(8,128)} fusion(f32[2,8,192,128]{3,2,1,0:T(8,128)} %get-tuple-element.85, f32[2,1024,192,8]{1,2,3,0:T(8,128)S(1)} %get-tuple-element.190, f32[2,8,192]{2,1,0:T(8,128)S(1)} %max.24, pred[192,1024]{1,0:T(8,128)(4,1)S(1)} %broadcast_compare_fusion.2, f32[2,8,192]{2,1,0:T(8,128)S(1)} %get-tuple-element.178, ...), kind=kOutput, calls=%fused_computation.68 | convolution fusion | flops 821821440 | bytes 16482304 | tf_op jit(solution)/shard_map/cond/branch_1_fun/kgrl,lkh->kgrh/dot_general | solution.py:22
  223.8 2.0 fusion.54
  226.3 1.2 convert_element_type.50
  (55 shorter events, 13.2 us)
Async XLA Ops:
  6.5 21.7 %copy-start = (bf16[64,32,2,256]{3,2,1,0:T(2,128)(2,1)S(1)}, bf16[64,32,2,256]{3,2,1,0:T(2,128)(2,1)}, u32[]{:S(2)}) copy-start(bf16[64,32,2,256]{3,2,1,0:T(2,128)(2,1)} %param.16) | copy-start | bytes 6291460
  6.5 35.7 %copy-start.4 = (s32[1,128,1]{1,2,0:T(1,128)S(1)}, s32[1,128,1]{1,2,0:T(1,128)}, u32[]{:S(2)}) copy-start(s32[1,128,1]{1,2,0:T(1,128)} %param.17) | copy-start | bytes 1540
  6.5 36.0 %copy-start.5 = (s32[1,768]{1,0:T(1,128)S(1)}, s32[1,768]{1,0:T(1,128)}, u32[]{:S(2)}) copy-start(s32[1,768]{1,0:T(1,128)} %param.19) | copy-start | bytes 9220
  6.5 96.3 %copy-start.3 = (bf16[1,192,2,256]{3,2,1,0:T(2,128)(2,1)S(1)}, bf16[1,192,2,256]{3,2,1,0:T(2,128)(2,1)}, u32[]{:S(2)}) copy-start(bf16[1,192,2,256]{3,2,1,0:T(2,128)(2,1)} %param.15) | copy-start | bytes 589828
  38.2 55.7 %all-to-all-start.1 = ((bf16[32,2,32,2,256]{4,2,3,1,0:T(8,128)(2,1)}), bf16[32,2,32,2,256]{4,2,3,1,0:T(8,128)(2,1)S(1)}, u32[]{:S(2)}, u32[]{:S(2)}) async-start(bf16[32,2,32,2,256]{4,2,3,1,0:T(8,128)(2,1)} %copy_select_fusion), calls=%async_computation.1 | async-start | bytes 4194304 | tf_op jit(solution)/shard_map/all_to_all | solution.py:117
  42.2 113.1 %all-gather.2.cloned.1.call-start = ((), (), s32[]{:S(2)}) async-start(), calls=%async_computation.2 | async-start | bytes 5242880 | tf_op jit(solution)/shard_map/all_gather | solution.py:120
  109.1 1.0 copy-start.2
  223.8 3.8 %copy-start.1 = (bf16[64,32,2,256]{3,2,1,0:T(2,128)(2,1)S(1)}, bf16[64,32,2,256]{3,2,1,0:T(2,128)(2,1)}, u32[]{:S(2)}) copy-start(bf16[64,32,2,256]{3,2,1,0:T(2,128)(2,1)} %param.16) | copy-start | bytes 6291460
Sparse Core Ops, SparseCore 0:
  110.2 45.1 all-gather.1
where the time goes:
time: 236 us; the launch traced here: 234 us
  waiting for transfers between devices  92 us (39%)
  other arithmetic  39.6 us (17%)
  matrix products  34.3 us (15%)
  local copies, waits for them, and re-layouts  30.2 us (13%)
  blocking collectives  17.8 us (8%)
  between operations  16.1 us (7%)
  starting transfers between devices  4.05 us (2%)
    all_to_all x1, waiting for transfers between devices, shards(): lax.all_to_all(found_pages, 'cache', split_axis=0, concat_axis=0, tiled=T...  51.3 us
    all_gather x1, waiting for transfers between devices, shards(): lax.all_gather(merged, 'ctx', axis=0, tiled=True)  40.7 us
    dot_general x4, matrix products, attend_rows(): jnp.einsum('kgrl,lkh->kgrh', weights.astype(jnp.bfloat16), key_rows[:, :,...  24.1 us
    all_to_all x1, blocking collectives, shards(): lax.all_to_all(requests, 'cache', split_axis=0, concat_axis=0, tiled=True)  17.8 us
    reduce_sum x4, other arithmetic, attend_rows(): row_sum = row_sum * factor + jnp.sum(weights, axis=-1)  17.7 us
    dot_general x4, matrix products, attend_rows(): jnp.einsum('rkgh,lkh->kgrl', queries, key_rows[:, :, :head_dim], preferre...  10.2 us
    select_n x2, other arithmetic, pick_pages(): jnp.take(flat_pages, jnp.minimum(target_slot, flat_pages.shape[0] - 1), a...  8.93 us
    gather x1, local copies, waits for them, and re-layouts, shards(): jnp.take(kv_store, jnp.maximum(lax.all_to_all(requests, 'cache', split_ax...  6.78 us
  transfers between devices with their start and end apart: 2, of which 2 were waited for; matrix products, arithmetic and copies ran while one was open for 1% of the time, Pallas kernels for 0%

commit v1 on v0

v1 whole, which is shorter than its diff:
```python
import functools
import math

import jax
import jax.numpy as jnp
from jax import lax
from jax.experimental import pallas as pl
from jax.experimental.pallas import tpu as pltpu
from jax.sharding import PartitionSpec as P

MESH = pl.DeviceIdType.MESH
EMPTY = -1e30
HIDDEN = -2e30
HALVES = 2


def kernel(
    dims, req, idx, rec_row, rec_col, store, fresh, queries, out,
    req_in, req_smem, sendbuf, kv, part, keep, q_all, m_all, l_all, acc_all,
    req_send, req_recv, smem_sem, page_send, page_recv, ctx_send, ctx_recv, *recvbuf,
):
    n, ctx_count, kv_heads, pages, page_len, rows, heads, hd = dims
    pieces = kv_heads * HALVES
    run = page_len // HALVES
    length = pages * run
    group = heads // kv_heads
    me = lax.axis_index("cache")
    c = lax.axis_index("ctx")

    barrier = pltpu.get_barrier_semaphore()

    def greet(k, _):
        pl.semaphore_signal(barrier, inc=1, device_id={"cache": lax.rem(me + k, n)}, device_id_type=MESH)
        return 0

    lax.fori_loop(1, n, greet, 0)
    for step in (1, ctx_count - 1):
        pl.semaphore_signal(barrier, inc=1, device_id={"ctx": lax.rem(c + step, ctx_count)}, device_id_type=MESH)
    pl.semaphore_wait(barrier, n + 1)

    def ask(k, _):
        d = lax.rem(me + k, n)
        pltpu.make_async_remote_copy(
            req.at[d], req_in.at[me], req_send, req_recv, device_id={"cache": d}, device_id_type=MESH
        ).start()
        return 0

    lax.fori_loop(1, n, ask, 0)
    req_in[me] = req[me]

    fresh_pos = rec_row[...]
    for half in range(HALVES):
        local = lax.broadcasted_iota(jnp.int32, (length, rows), 0)
        pos = (local // run) * page_len + half * run + local % run
        hit = jnp.where(pos == fresh_pos, 1.0, 0.0)
        covered = jnp.sum(hit, axis=1, keepdims=True)
        keep[half] = jnp.broadcast_to(1.0 - covered, (length, 2 * hd)).astype(jnp.bfloat16)
        one_hot = hit.astype(jnp.bfloat16)
        for k in range(kv_heads):
            part[k * HALVES + half] = jnp.dot(
                one_hot, fresh[k], preferred_element_type=jnp.float32
            ).astype(jnp.bfloat16)
    for g in range(heads):
        q_all[g] = queries[:, g * hd : (g + 1) * hd]
    m_all[...] = jnp.full(m_all.shape, EMPTY, jnp.float32)
    l_all[...] = jnp.zeros(l_all.shape, jnp.float32)
    acc_all[...] = jnp.zeros(acc_all.shape, jnp.float32)

    others = req_in.at[pl.ds(0, n - 1)]
    pltpu.make_async_copy(others, others, req_recv).wait()
    to_smem = pltpu.make_async_copy(req_in, req_smem, smem_sem)
    to_smem.start()
    to_smem.wait()

    for q in range(pieces):

        def fill(d, q=q):
            for r in range(2):
                sendbuf[q, d, r] = store[req_smem[d, 0, r] * pieces + q]

        def give(k, _, q=q, fill=fill):
            d = lax.rem(me + k, n)
            fill(d)
            pltpu.make_async_remote_copy(
                sendbuf.at[q, d], recvbuf[q].at[me], page_send.at[q], page_recv.at[q],
                device_id={"cache": d}, device_id_type=MESH,
            ).start()
            return 0

        lax.fori_loop(1, n, give, 0)
        for r in range(2):
            recvbuf[q][me, r] = store[req_smem[me, 0, r] * pieces + q]

    factor = hd**-0.5 * math.log2(math.e)

    def attend(q, block, own):
        def one(g, _):
            keys, values = kv[q * ctx_count + block, :, :hd], kv[q * ctx_count + block, :, hd:]
            scores = lax.dot_general(
                q_all[g], keys, (((1,), (1,)), ((), ())), preferred_element_type=jnp.float32
            )
            if own:
                local = lax.broadcasted_iota(jnp.int32, (rows, length), 1)
                pos = (local // run) * page_len + (q % HALVES) * run + local % run
                scores = jnp.where(pos <= rec_col[...], scores, HIDDEN)
            m_old = m_all[g]
            m_new = jnp.maximum(m_old, jnp.max(scores, axis=1, keepdims=True))
            alpha = jnp.exp2((m_old - m_new) * factor)
            weights = jnp.exp2((scores - m_new[:, :1]) * factor)
            l_all[g] = l_all[g] * alpha + jnp.sum(weights, axis=1, keepdims=True)
            acc_all[g] = acc_all[g] * alpha + jnp.dot(
                weights.astype(jnp.bfloat16), values, preferred_element_type=jnp.float32
            )
            m_all[g] = m_new
            return 0

        k = q // HALVES
        lax.fori_loop(k * group, (k + 1) * group, one, 0)

    def along(q, block, sem, to):
        ref = kv.at[q * ctx_count + block]
        return pltpu.make_async_remote_copy(
            ref, ref, ctx_send.at[q, sem], ctx_recv.at[q, block], device_id={"ctx": to}, device_id_type=MESH
        )

    for q in range(pieces):
        others = recvbuf[q].at[pl.ds(0, n - 1)]
        pltpu.make_async_copy(others, others, page_recv.at[q]).wait()

        def place(j, _, q=q):
            at = idx[j]
            spot = pl.ds(pl.multiple_of(j * run, run), run)
            page = recvbuf[q][at // 2, at % 2]
            kv[q * ctx_count + c, spot, :] = page * keep[q % HALVES, spot, :] + part[q, spot, :]
            return 0

        lax.fori_loop(0, pages, place, 0)

        @pl.when(c < ctx_count - 1)
        def _():
            along(q, c, 0, c + 1).start()

        @pl.when(c == 0)
        def _():
            along(q, c, 1, ctx_count - 1).start()

        attend(q, c, True)
        for t in range(ctx_count - 1):

            @pl.when(t < c)
            def _(t=t, q=q):
                last = c // 3
                block = last * ((3 - t) % 3) + (1 - last) * (c - 1 - t)
                along(q, block, 0, c).wait_recv()
                if t == 0:

                    @pl.when(c >= 2)
                    def _():
                        along(q, block, 2, 5 - c).start()

                attend(q, block, False)

    for g in range(heads):
        out[:, g * hd : (g + 1) * hd] = (acc_all[g] / l_all[g]).astype(out.dtype)

    def sent(q, sem):
        pltpu.make_async_copy(kv.at[0], kv.at[0], ctx_send.at[q, sem]).wait()

    pltpu.make_async_copy(req.at[pl.ds(0, n - 1)], req.at[pl.ds(0, n - 1)], req_send).wait()
    for q in range(pieces):
        most = sendbuf.at[q, pl.ds(0, n - 1)]
        pltpu.make_async_copy(most, most, page_send.at[q]).wait()

        @pl.when(c < ctx_count - 1)
        def _():
            sent(q, 0)

        @pl.when(c == 0)
        def _():
            sent(q, 1)

        @pl.when(c >= 2)
        def _():
            sent(q, 2)


def shards(queries, fresh_kv, kv_store, page_owner, page_slot, rec_index):
    n, ctx_count = lax.axis_size("cache"), lax.axis_size("ctx")
    c = lax.axis_index("ctx")
    rows, kv_heads, hd = queries.shape[1], fresh_kv.shape[2], fresh_kv.shape[3] // 2
    heads = queries.shape[2] // hd
    slots, page_len = kv_store.shape[:2]
    pages = page_owner.shape[1] // ctx_count
    pieces, run = kv_heads * HALVES, page_len // HALVES

    owners = lax.dynamic_slice_in_dim(page_owner[0, :, 0], c * pages, pages)
    slot_ids = lax.dynamic_slice_in_dim(page_slot[0], c * pages, pages)
    rec = lax.dynamic_slice_in_dim(rec_index[0], c * rows, rows)
    order = lax.iota(jnp.int32, pages)
    named = owners[None, :] == lax.iota(jnp.int32, n)[:, None]
    coded = (order * slots + slot_ids)[None, :]
    none = pages * slots
    first = jnp.min(jnp.where(named, coded, none), axis=1) % slots
    last = jnp.max(jnp.where(named, coded, 0), axis=1) % slots
    lane = lax.broadcasted_iota(jnp.int32, (n, 1, 128), 2)
    req = jnp.where(lane == 0, first[:, None, None], last[:, None, None])
    same = owners[None, :] == owners[:, None]
    earliest = jnp.min(jnp.where(same, order[None, :], pages), axis=1)
    idx = owners * 2 + (earliest != order).astype(jnp.int32)

    store = kv_store.transpose(0, 2, 1, 3).reshape(slots * pieces, run, 2 * hd)
    fresh = fresh_kv[0].transpose(1, 0, 2)
    dims = (n, ctx_count, kv_heads, pages, page_len, rows, heads, hd)
    bf16, f32 = jnp.bfloat16, jnp.float32
    vmem, smem = pl.BlockSpec(memory_space=pltpu.VMEM), pl.BlockSpec(memory_space=pltpu.SMEM)
    dma = pltpu.SemaphoreType.DMA
    result = pl.pallas_call(
        functools.partial(kernel, dims),
        out_shape=jax.ShapeDtypeStruct((rows, heads * hd), bf16),
        in_specs=[vmem, smem, vmem, vmem, vmem, vmem, vmem],
        out_specs=vmem,
        scratch_shapes=[
            pltpu.VMEM((n, 1, 128), jnp.int32),
            pltpu.SMEM((n, 1, 128), jnp.int32),
            pltpu.VMEM((pieces, n, 2, run, 2 * hd), bf16),
            pltpu.VMEM((pieces * ctx_count, pages * run, 2 * hd), bf16),
            pltpu.VMEM((pieces, pages * run, 2 * hd), bf16),
            pltpu.VMEM((HALVES, pages * run, 2 * hd), bf16),
            pltpu.VMEM((heads, rows, hd), bf16),
            pltpu.VMEM((heads, rows, 128), f32),
            pltpu.VMEM((heads, rows, 128), f32),
            pltpu.VMEM((heads, rows, hd), f32),
            dma, dma, dma,
            dma((pieces,)), dma((pieces,)),
            dma((pieces, 3)), dma((pieces, ctx_count)),
            *[pltpu.VMEM((n, 2, run, 2 * hd), bf16) for _ in range(pieces)],
        ],
        compiler_params=pltpu.CompilerParams(
            collective_id=0, has_side_effects=True, vmem_limit_bytes=48 * 1024 * 1024
        ),
    )(req, idx, rec[None, :], rec[:, None], store, fresh, queries[0])
    return result[None]


def solution(mesh):
    in_specs = (
        P("cache", "ctx", "head"),
        P("cache", "ctx", "head", None),
        P("cache", None, "head", None),
        P("cache", None, None),
        P("cache", None),
        P("cache", None),
    )
    out_specs = P("cache", "ctx", "head")
    return jax.shard_map(shards, mesh=mesh, in_specs=in_specs, out_specs=out_specs, check_vma=False)
```

time: 236 us -> 112 us (0.47)
  Pallas kernels: 0 us -> 104 us
  waiting for transfers between devices: 92 us -> 0 us
  other arithmetic: 39.6 us -> 1.8 us
  matrix products: 34.3 us -> 0 us
  local copies, waits for them, and re-layouts: 30.2 us -> 4.95 us
  blocking collectives: 17.8 us -> 0 us
  between operations: 16.1 us -> 0.07 us
  starting transfers between devices: 4.05 us -> 0 us
    pallas_call x0 -> x1, Pallas kernels: none -> 104 us  [shards(): pl.pallas_call(functools.partial(kernel, dims), out_shape=jax.ShapeDtypeS...]
    all_to_all x1 -> x0, waiting for transfers between devices: 51.3 us -> none  [shards(): lax.all_to_all(found_pages, 'cache', split_axis=0, concat_axis=0, tiled=T...]
    all_gather x1 -> x0, waiting for transfers between devices: 40.7 us -> none  [shards(): lax.all_gather(merged, 'ctx', axis=0, tiled=True)]
    dot_general x8 -> x0, matrix products: 34.3 us -> none  [the longest x4 24.1 us: attend_rows(): jnp.einsum('kgrl,lkh->kgrh', weights.astype(jnp.bfloat16), key_rows[:, :,...]
    reduce_sum x5 -> x0, other arithmetic: 17.9 us -> none  [the longest x4 17.7 us: attend_rows(): row_sum = row_sum * factor + jnp.sum(weights, axis=-1)]
    all_to_all x1 -> x0, blocking collectives: 17.8 us -> none  [shards(): lax.all_to_all(requests, 'cache', split_axis=0, concat_axis=0, tiled=True)]
    select_n x5 -> x2, other arithmetic: 12.2 us -> 0.14 us  [the longest x1 0.13 us: shards(): req = jnp.where(lane == 0, first[:, None, None], last[:, None, None])]
    gather x3 -> x0, local copies, waits for them, and re-layouts: 7.47 us -> none  [the longest x1 6.78 us: shards(): jnp.take(kv_store, jnp.maximum(lax.all_to_all(requests, 'cache', split_ax...]
  transfers between devices with their start and end apart: 2 -> 0, of which waited for: 2 -> 0; matrix products, arithmetic and copies ran while one was open for 1% -> 0% of each run, Pallas kernels for 0% -> 0%
where the time goes in v1:
time: 112 us; the launch traced here: 111 us
  Pallas kernels  104 us (93%)
  local copies, waits for them, and re-layouts  4.95 us (4%)
  other arithmetic  1.8 us (2%)
    pallas_call x1, Pallas kernels, shards(): pl.pallas_call(functools.partial(kernel, dims), out_shape=jax.ShapeDtypeS...  104 us

profile of v1, /device:TPU:24, one launch (start us, length us, event | category | flops | bytes accessed | tf_op | source)
XLA Modules:
  0.0 110.6 jit_solution(16139678665621328613)
XLA Ops:
  0.0 0.0 copy-start
  0.0 0.7 fusion.2
  0.7 0.7 fusion
  1.5 0.2 select_reduce_fusion.2
  1.7 0.7 fusion.3.idx
  2.4 0.0 copy-done
  2.4 0.1 fusion.6
  2.5 0.1 constant_dynamic-slice_fusion.rec_row
  2.6 0.1 broadcast_select_fusion.req
  2.7 0.1 copy.14.rec_col
  2.8 1.0 copy.16
  3.8 0.0 copy-start.1
  3.8 2.1 %copy.12 = bf16[64,2,32,256]{3,2,1,0:T(8,128)(2,1)S(1)} copy(bf16[64,2,32,256]{3,1,2,0:T(2,128)(2,1)} %bitcast.21) | data formatting | bytes 4194304 | tf_op jit(solution)/shard_map/transpose | solution.py:211
  5.9 0.0 copy-done.1
  5.9 103.8 %shard_map.64 = bf16[192,2048]{1,0:T(8,128)(2,1)S(1)} custom-call(s32[32,1,128]{2,1,0:T(1,128)S(1)} %broadcast_select_fusion.req, s32[32]{0:T(128)S(1)} %fusion.3.idx, s32[1,192]{1,0:T(1,128)S(1)} %constant_dynamic-slice_fusion.rec_row, s32[192,1]{1,0:T(8,128)S(1)} %copy.14.rec_col, bf16[256,16,256]{2,1,0:T(8,128)(2,1)S(1)} %bitcast.17, ...), custom_call_target="tpu_custom_call" | custom-call | tf_op jit(solution)/shard_map/pallas_call | solution.py:217
  109.7 0.9 copy.18
  (2 shorter events, 0.0 us)
Async XLA Ops:
  0.0 2.4 %copy-start = (s32[1,768]{1,0:T(1,128)S(1)}, s32[1,768]{1,0:T(1,128)}, u32[]{:S(2)}) copy-start(s32[1,768]{1,0:T(1,128)} %param.11) | copy-start | bytes 9220
  3.8 2.1 %copy-start.1 = (bf16[1,192,2048]{2,1,0:T(8,128)(2,1)S(1)}, bf16[1,192,2048]{2,1,0:T(8,128)(2,1)}, u32[]{:S(2)}) copy-start(bf16[1,192,2048]{2,1,0:T(8,128)(2,1)} %param.6) | copy-start | bytes 2359300

commit v2 on v1

v2 whole, which is shorter than its diff:
```python
import functools
import math

import jax
import jax.numpy as jnp
from jax import lax
from jax.experimental import pallas as pl
from jax.experimental.pallas import tpu as pltpu
from jax.sharding import PartitionSpec as P

MESH = pl.DeviceIdType.MESH
EMPTY = -1e30
HIDDEN = -2e30
HALVES = 2


def kernel(
    dims, req, idx, rec_row, rec_tiled, store, fresh, queries, out,
    req_in, req_smem, sendbuf, kv, v_rows, part, keep, stack, q_t, m_all, l_all, acc_all,
    req_send, req_recv, smem_sem, page_send, page_recv, ctx_send, ctx_recv, *recvbuf,
):
    n, ctx_count, kv_heads, pages, page_len, rows, heads, hd = dims
    pieces = kv_heads * HALVES
    run = page_len // HALVES
    length = pages * run
    group = heads // kv_heads
    me = lax.axis_index("cache")
    c = lax.axis_index("ctx")

    barrier = pltpu.get_barrier_semaphore()

    def greet(k, _):
        pl.semaphore_signal(barrier, inc=1, device_id={"cache": lax.rem(me + k, n)}, device_id_type=MESH)
        return 0

    lax.fori_loop(1, n, greet, 0)
    for step in (1, ctx_count - 1):
        pl.semaphore_signal(barrier, inc=1, device_id={"ctx": lax.rem(c + step, ctx_count)}, device_id_type=MESH)
    pl.semaphore_wait(barrier, n + 1)

    def ask(k, _):
        d = lax.rem(me + k, n)
        pltpu.make_async_remote_copy(
            req.at[d], req_in.at[me], req_send, req_recv, device_id={"cache": d}, device_id_type=MESH
        ).start()
        return 0

    lax.fori_loop(1, n, ask, 0)
    req_in[me] = req[me]

    others = req_in.at[pl.ds(0, n - 1)]
    pltpu.make_async_copy(others, others, req_recv).wait()
    to_smem = pltpu.make_async_copy(req_in, req_smem, smem_sem)
    to_smem.start()
    to_smem.wait()

    for q in range(pieces):

        def fill(d, q=q):
            for r in range(2):
                sendbuf[q, d, r] = store[req_smem[d, 0, r] * pieces + q]

        def give(k, _, q=q, fill=fill):
            d = lax.rem(me + k, n)
            fill(d)
            pltpu.make_async_remote_copy(
                sendbuf.at[q, d], recvbuf[q].at[me], page_send.at[q], page_recv.at[q],
                device_id={"cache": d}, device_id_type=MESH,
            ).start()
            return 0

        lax.fori_loop(1, n, give, 0)
        for r in range(2):
            recvbuf[q][me, r] = store[req_smem[me, 0, r] * pieces + q]

    fresh_pos = rec_row[...]
    for half in range(HALVES):
        local = lax.broadcasted_iota(jnp.int32, (length, rows), 0)
        pos = (local // run) * page_len + half * run + local % run
        hit = jnp.where(pos == fresh_pos, 1.0, 0.0)
        covered = jnp.sum(hit, axis=1, keepdims=True)
        keep[half] = jnp.broadcast_to(1.0 - covered, (length, 2 * hd)).astype(jnp.bfloat16)
        one_hot = hit.astype(jnp.bfloat16)
        for k in range(kv_heads):
            part[k * HALVES + half] = jnp.dot(
                one_hot, fresh[k], preferred_element_type=jnp.float32
            ).astype(jnp.bfloat16)

    columns = group * rows
    for g in range(heads):
        at = (g % group) * rows
        stack[g // group, at : at + rows, :] = queries[:, g * hd : (g + 1) * hd]
    for k in range(kv_heads):
        for at in range(0, columns, 128):
            block = stack[k, at : at + 128, :].astype(jnp.float32)
            q_t[k, :, at : at + 128] = block.T.astype(jnp.bfloat16)
    m_all[...] = jnp.full(m_all.shape, EMPTY, jnp.float32)
    l_all[...] = jnp.zeros(l_all.shape, jnp.float32)
    acc_all[...] = jnp.zeros(acc_all.shape, jnp.float32)

    factor = hd**-0.5 * math.log2(math.e)

    def attend(q, block, own):
        k = q // HALVES
        at = q * ctx_count + block
        keys = kv[at, :length, :]
        values = jnp.concatenate(
            [kv[at, length + i : length + i + 128, :] for i in range(0, length, 128)], axis=1
        )
        scores = jnp.dot(keys, q_t[k], preferred_element_type=jnp.float32)
        if own:
            local = lax.broadcasted_iota(jnp.int32, (length, 1), 0)
            pos = (local // run) * page_len + (q % HALVES) * run + local % run
            scores = jnp.where(pos <= rec_tiled[...], scores, HIDDEN)
        m_old = m_all[k]
        m_new = jnp.maximum(m_old, jnp.max(scores, axis=0, keepdims=True))
        alpha = jnp.exp2((m_old - m_new) * factor)
        weights = jnp.exp2((scores - m_new[:1]) * factor)
        l_all[k] = l_all[k] * alpha + jnp.sum(weights, axis=0, keepdims=True)
        acc_all[k] = acc_all[k] * alpha[:1] + jnp.dot(
            values, weights.astype(jnp.bfloat16), preferred_element_type=jnp.float32
        )
        m_all[k] = m_new

    halves = (pl.ds(0, length), pl.ds(length, length))
    whole = pl.ds(0, 2 * length)

    def along(q, block, span, sem, flag, to):
        ref = kv.at[q * ctx_count + block, span]
        return pltpu.make_async_remote_copy(
            ref, ref, ctx_send.at[q, sem], ctx_recv.at[q, block, flag],
            device_id={"ctx": to}, device_id_type=MESH,
        )

    for q in range(pieces):
        others = recvbuf[q].at[pl.ds(0, n - 1)]
        pltpu.make_async_copy(others, others, page_recv.at[q]).wait()

        def place(j, _, q=q):
            at = idx[j]
            spot = pl.ds(pl.multiple_of(j * run, run), run)
            page = recvbuf[q][at // 2, at % 2] * keep[q % HALVES, spot, :] + part[q, spot, :]
            kv[q * ctx_count + c, spot, :] = page[:, :hd]
            v_rows[spot, :] = page[:, hd:]
            return 0

        lax.fori_loop(0, pages, place, 0)
        for i in range(0, length, 128):
            block = v_rows[i : i + 128, :].astype(jnp.float32)
            kv[q * ctx_count + c, length + i : length + i + 128, :] = block.T.astype(jnp.bfloat16)

        @pl.when(c == 0)
        def _(q=q):
            along(q, 0, whole, 1, 0, 3).start()
            along(q, 0, whole, 0, 0, 1).start()

        @pl.when(c == 1)
        def _(q=q):
            along(q, 1, halves[1], 2, 1, 0).start()
            along(q, 1, halves[0], 0, 0, 2).start()
            along(q, 1, halves[1], 1, 1, 2).start()

        @pl.when(c == 2)
        def _(q=q):
            along(q, 2, whole, 0, 0, 3).start()

        attend(q, c, True)

        @pl.when(c == 0)
        def _(q=q):
            along(q, 1, halves[1], 2, 1, 0).wait_recv()
            along(q, 1, halves[1], 2, 1, 3).start()

        def earlier(t, _, q=q):
            last = c // 3
            block = last * ((3 - t) % 3) + (1 - last) * (c - 1 - t)

            @pl.when(block == 1)
            def _():
                along(q, 1, halves[0], 0, 0, c).wait_recv()

                @pl.when(c == 2)
                def _():
                    along(q, 1, halves[0], 1, 0, 3).start()

                along(q, 1, halves[1], 1, 1, c).wait_recv()

            @pl.when(block != 1)
            def _():
                along(q, block, whole, 0, 0, c).wait_recv()

                @pl.when((c == 3) & (block == 0))
                def _():
                    along(q, 0, whole, 0, 0, 2).start()

            attend(q, block, False)
            return 0

        lax.fori_loop(0, c, earlier, 0)

    for k in range(kv_heads):
        for at in range(0, columns, 128):
            span = slice(at, at + 128)
            stack[k, span, :] = (acc_all[k, :, span] / l_all[k, :1, span]).T.astype(jnp.bfloat16)
    for g in range(heads):
        at = (g % group) * rows
        out[:, g * hd : (g + 1) * hd] = stack[g // group, at : at + rows, :]

    pltpu.make_async_copy(req.at[pl.ds(0, n - 1)], req.at[pl.ds(0, n - 1)], req_send).wait()
    for q in range(pieces):
        most = sendbuf.at[q, pl.ds(0, n - 1)]
        pltpu.make_async_copy(most, most, page_send.at[q]).wait()

        @pl.when(c == 0)
        def _(q=q):
            along(q, 0, whole, 0, 0, 1).wait_send()
            along(q, 0, whole, 1, 0, 3).wait_send()
            along(q, 1, halves[1], 2, 1, 3).wait_send()

        @pl.when(c == 1)
        def _(q=q):
            along(q, 1, halves[0], 0, 0, 2).wait_send()
            along(q, 1, halves[1], 1, 1, 2).wait_send()
            along(q, 1, halves[1], 2, 1, 0).wait_send()

        @pl.when(c == 2)
        def _(q=q):
            along(q, 2, whole, 0, 0, 3).wait_send()
            along(q, 1, halves[0], 1, 0, 3).wait_send()

        @pl.when(c == 3)
        def _(q=q):
            along(q, 0, whole, 0, 0, 2).wait_send()


def shards(queries, fresh_kv, kv_store, page_owner, page_slot, rec_index):
    n, ctx_count = lax.axis_size("cache"), lax.axis_size("ctx")
    c = lax.axis_index("ctx")
    rows, kv_heads, hd = queries.shape[1], fresh_kv.shape[2], fresh_kv.shape[3] // 2
    heads = queries.shape[2] // hd
    slots, page_len = kv_store.shape[:2]
    pages = page_owner.shape[1] // ctx_count
    pieces, run = kv_heads * HALVES, page_len // HALVES

    owners = lax.dynamic_slice_in_dim(page_owner[0, :, 0], c * pages, pages)
    slot_ids = lax.dynamic_slice_in_dim(page_slot[0], c * pages, pages)
    rec = lax.dynamic_slice_in_dim(rec_index[0], c * rows, rows)
    order = lax.iota(jnp.int32, pages)
    named = owners[None, :] == lax.iota(jnp.int32, n)[:, None]
    coded = (order * slots + slot_ids)[None, :]
    none = pages * slots
    first = jnp.min(jnp.where(named, coded, none), axis=1) % slots
    last = jnp.max(jnp.where(named, coded, 0), axis=1) % slots
    lane = lax.broadcasted_iota(jnp.int32, (n, 1, 128), 2)
    req = jnp.where(lane == 0, first[:, None, None], last[:, None, None])
    same = owners[None, :] == owners[:, None]
    earliest = jnp.min(jnp.where(same, order[None, :], pages), axis=1)
    idx = owners * 2 + (earliest != order).astype(jnp.int32)

    store = kv_store.transpose(0, 2, 1, 3).reshape(slots * pieces, run, 2 * hd)
    fresh = fresh_kv[0].transpose(1, 0, 2)
    columns = heads // kv_heads * rows
    dims = (n, ctx_count, kv_heads, pages, page_len, rows, heads, hd)
    bf16, f32 = jnp.bfloat16, jnp.float32
    vmem, smem = pl.BlockSpec(memory_space=pltpu.VMEM), pl.BlockSpec(memory_space=pltpu.SMEM)
    dma = pltpu.SemaphoreType.DMA
    result = pl.pallas_call(
        functools.partial(kernel, dims),
        out_shape=jax.ShapeDtypeStruct((rows, heads * hd), bf16),
        in_specs=[vmem, smem, vmem, vmem, vmem, vmem, vmem],
        out_specs=vmem,
        scratch_shapes=[
            pltpu.VMEM((n, 1, 128), jnp.int32),
            pltpu.SMEM((n, 1, 128), jnp.int32),
            pltpu.VMEM((pieces, n, 2, run, 2 * hd), bf16),
            pltpu.VMEM((pieces * ctx_count, 2 * pages * run, hd), bf16),
            pltpu.VMEM((pages * run, hd), bf16),
            pltpu.VMEM((pieces, pages * run, 2 * hd), bf16),
            pltpu.VMEM((HALVES, pages * run, 2 * hd), bf16),
            pltpu.VMEM((kv_heads, columns, hd), bf16),
            pltpu.VMEM((kv_heads, hd, columns), bf16),
            pltpu.VMEM((kv_heads, 8, columns), f32),
            pltpu.VMEM((kv_heads, 8, columns), f32),
            pltpu.VMEM((kv_heads, hd, columns), f32),
            dma, dma, dma,
            dma((pieces,)), dma((pieces,)),
            dma((pieces, 3)), dma((pieces, ctx_count, 2)),
            *[pltpu.VMEM((n, 2, run, 2 * hd), bf16) for _ in range(pieces)],
        ],
        compiler_params=pltpu.CompilerParams(
            collective_id=0, has_side_effects=True, vmem_limit_bytes=48 * 1024 * 1024
        ),
    )(req, idx, rec[None, :], jnp.tile(rec, heads // kv_heads)[None, :], store, fresh, queries[0])
    return result[None]


def solution(mesh):
    in_specs = (
        P("cache", "ctx", "head"),
        P("cache", "ctx", "head", None),
        P("cache", None, "head", None),
        P("cache", None, None),
        P("cache", None),
        P("cache", None),
    )
    out_specs = P("cache", "ctx", "head")
    return jax.shard_map(shards, mesh=mesh, in_specs=in_specs, out_specs=out_specs, check_vma=False)
```

time: 112 us -> 88.2 us (0.79)
  Pallas kernels: 104 us -> 80 us
    pallas_call x1, Pallas kernels: 104 us -> 80 us  [shards(): pl.pallas_call(functools.partial(kernel, dims), out_shape=jax.ShapeDtypeS...]
where the time goes in v2:
time: 88.2 us; the launch traced here: 87.3 us
  Pallas kernels  80 us (91%)
  local copies, waits for them, and re-layouts  5.54 us (6%)
  other arithmetic  1.78 us (2%)
    pallas_call x1, Pallas kernels, shards(): pl.pallas_call(functools.partial(kernel, dims), out_shape=jax.ShapeDtypeS...  80 us
    unnamed x6, local copies, waits for them, and re-layouts  2.52 us
    transpose x1, local copies, waits for them, and re-layouts, shards(): store = kv_store.transpose(0, 2, 1, 3).reshape(slots * pieces, run, 2 * hd)  2.13 us

profile of v2, /device:TPU:24, one launch (start us, length us, event | category | flops | bytes accessed | tf_op | source)
XLA Modules:
  0.0 87.3 jit_solution(15286538050471985758)
XLA Ops:
  0.0 0.0 copy-start
  0.0 0.7 copy-done
  0.7 0.1 constant_dynamic-slice_fusion.rec_row
  0.8 0.7 fusion.2
  1.5 0.7 fusion
  2.2 0.2 select_reduce_fusion.2
  2.4 0.7 fusion.3.idx
  3.2 0.1 broadcast_in_dim_tile.3.rec_tiled
  3.2 0.1 broadcast_select_fusion.req
  3.4 1.0 %copy.12 = bf16[1,192,2,256]{3,1,2,0:T(8,128)(2,1)S(1)} copy(bf16[1,192,2,256]{3,2,1,0:T(2,128)(2,1)} %param.7) | data formatting | bytes 393216 | tf_op args[1]
  4.3 0.0 copy-start.1
  4.3 2.1 %copy.9 = bf16[64,2,32,256]{3,2,1,0:T(8,128)(2,1)S(1)} copy(bf16[64,2,32,256]{3,1,2,0:T(2,128)(2,1)} %bitcast.21) | data formatting | bytes 4194304 | tf_op jit(solution)/shard_map/transpose | solution.py:260
  6.5 0.0 copy-done.1
  6.5 80.0 %shard_map.64 = bf16[192,2048]{1,0:T(8,128)(2,1)S(1)} custom-call(s32[32,1,128]{2,1,0:T(1,128)S(1)} %broadcast_select_fusion.req, s32[32]{0:T(128)S(1)} %fusion.3.idx, s32[1,192]{1,0:T(1,128)S(1)} %constant_dynamic-slice_fusion.rec_row, s32[1,1536]{1,0:T(1,128)S(1)} %broadcast_in_dim_tile.3.rec_tiled, bf16[256,16,256]{2,1,0:T(8,128)(2,1)S(1)} %bitcast.16, ...), custom_call_target="tpu_custom_call" | custom-call | tf_op jit(solution)/shard_map/pallas_call | solution.py:267
  86.5 0.9 %copy.14 = bf16[1,192,2048]{2,1,0:T(8,128)(2,1)} copy(bf16[1,192,2048]{2,1,0:T(8,128)(2,1)S(1)} %bitcast.17) | data formatting | bytes 1572864
  (3 shorter events, 0.0 us)
Async XLA Ops:
  0.0 0.7 copy-start
  4.3 2.2 %copy-start.1 = (bf16[1,192,2048]{2,1,0:T(8,128)(2,1)S(1)}, bf16[1,192,2048]{2,1,0:T(8,128)(2,1)}, u32[]{:S(2)}) copy-start(bf16[1,192,2048]{2,1,0:T(8,128)(2,1)} %param.6) | copy-start | bytes 2359300

commit v3 on v2

v3 whole, which is shorter than its diff:
```python
import functools
import math

import jax
import jax.numpy as jnp
from jax import lax
from jax.experimental import pallas as pl
from jax.experimental.pallas import tpu as pltpu
from jax.sharding import PartitionSpec as P

MESH = pl.DeviceIdType.MESH
EMPTY = -1e30
HIDDEN = -2e30
HALVES = 2


def kernel(
    dims, owner_col, slot_row, rec_in, raw_in, fresh_in, queries_in, out,
    req, req_in, req_smem, idx_rows, idx, raw, fresh_raw, queries, store, sendbuf, kv, v_rows, rec_tiled,
    fresh, part, keep, stack, q_t, m_all, l_all, acc_all,
    load_sem, req_send, req_recv, smem_sem, page_send, page_recv, ctx_send, ctx_recv, *recvbuf,
):
    n, ctx_count, kv_heads, slots, pages, page_len, rows, heads, hd = dims
    parts = kv_heads * HALVES
    pieces = parts * 2
    run = page_len // HALVES
    length = pages * run
    group = heads // kv_heads
    columns = group * rows
    pages_all = pages * ctx_count
    i32 = jnp.int32
    me = lax.axis_index("cache")
    c = lax.axis_index("ctx")

    barrier = pltpu.get_barrier_semaphore()

    def greet(k, _):
        pl.semaphore_signal(barrier, inc=1, device_id={"cache": lax.rem(me + k, n)}, device_id_type=MESH)
        return 0

    lax.fori_loop(1, n, greet, 0)
    for step in (1, ctx_count - 1):
        pl.semaphore_signal(barrier, inc=1, device_id={"ctx": lax.rem(c + step, ctx_count)}, device_id_type=MESH)

    loads = [
        pltpu.make_async_copy(src, dst, load_sem.at[i])
        for i, (src, dst) in enumerate(((raw_in, raw), (fresh_in, fresh_raw), (queries_in, queries)))
    ]
    for load in loads:
        load.start()

    a = lax.broadcasted_iota(i32, (pages_all, pages_all), 0)
    b = lax.broadcasted_iota(i32, (pages_all, pages_all), 1)
    owner_of_a = jnp.broadcast_to(owner_col[...], (pages_all, pages_all))
    owner_row = jnp.sum(jnp.where(a == b, owner_of_a, 0), axis=0, keepdims=True)
    low = c * pages
    before = (owner_of_a == owner_row) & (a < b) & (a >= low)
    second = jnp.max(jnp.where(before, 1, 0), axis=0, keepdims=True)
    idx_rows[...] = jnp.broadcast_to(owner_row * 2 + second, idx_rows.shape)
    to_idx = pltpu.make_async_copy(idx_rows, idx, smem_sem.at[0])
    to_idx.start()

    shard = lax.broadcasted_iota(i32, (n, pages_all), 0)
    place_of = lax.broadcasted_iota(i32, (n, pages_all), 1)
    named = (shard == owner_row) & (place_of >= low) & (place_of < low + pages)
    coded = (place_of * slots + slot_row[...]).astype(jnp.float32)
    first = jnp.min(jnp.where(named, coded, float(pages_all * slots)), axis=1, keepdims=True)
    final = jnp.max(jnp.where(named, coded, 0.0), axis=1, keepdims=True)
    asked = jnp.where(place_of == 0, first, final).astype(i32) % slots
    for d in range(n):
        req[d] = asked[d : d + 1, :]

    loads[0].wait()

    def split(p, _):
        store[pl.ds(p * kv_heads, kv_heads)] = jnp.swapaxes(raw[p], 0, 1)
        return 0

    lax.fori_loop(0, slots, split, 0)
    to_idx.wait()
    pl.semaphore_wait(barrier, n + 1)

    def ask(k, _):
        d = lax.rem(me + k, n)
        pltpu.make_async_remote_copy(
            req.at[d], req_in.at[me], req_send, req_recv, device_id={"cache": d}, device_id_type=MESH
        ).start()
        return 0

    lax.fori_loop(1, n, ask, 0)
    req_in[me] = req[me]

    others = req_in.at[pl.ds(0, n - 1)]
    pltpu.make_async_copy(others, others, req_recv).wait()
    to_smem = pltpu.make_async_copy(req_in, req_smem, smem_sem.at[1])
    to_smem.start()
    to_smem.wait()

    def piece_of(q):
        half, which = q // 2 % HALVES, q % 2
        return q // (2 * HALVES), slice(half * run, (half + 1) * run), slice(which * hd, (which + 1) * hd)

    for q in range(pieces):
        k, span, lanes = piece_of(q)

        def page(d, r, k=k, span=span, lanes=lanes):
            return store[req_smem[d, 0, r] * kv_heads + k, span, lanes]

        def give(step, _, q=q, page=page):
            d = lax.rem(me + step, n)
            for r in range(2):
                sendbuf[q, d, r] = page(d, r)
            pltpu.make_async_remote_copy(
                sendbuf.at[q, d], recvbuf[q].at[me], page_send.at[q], page_recv.at[q],
                device_id={"cache": d}, device_id_type=MESH,
            ).start()
            return 0

        lax.fori_loop(1, n, give, 0)
        for r in range(2):
            recvbuf[q][me, r] = page(me, r)

    fresh_pos = jnp.zeros((1, rows), i32)
    for other in range(ctx_count):
        theirs = rec_in[:, other * rows : (other + 1) * rows]
        fresh_pos = jnp.where(c == other, theirs, fresh_pos)
    for g in range(group):
        rec_tiled[:, g * rows : (g + 1) * rows] = fresh_pos
    loads[1].wait()
    by_head = jnp.swapaxes(fresh_raw[...], 0, 1)
    for k in range(kv_heads):
        fresh[k] = by_head[k]
    loads[2].wait()
    for half in range(HALVES):
        local = lax.broadcasted_iota(jnp.int32, (length, rows), 0)
        pos = (local // run) * page_len + half * run + local % run
        hit = jnp.where(pos == fresh_pos, 1.0, 0.0)
        covered = jnp.sum(hit, axis=1, keepdims=True)
        keep[half] = jnp.broadcast_to(1.0 - covered, (length, hd)).astype(jnp.bfloat16)
        one_hot = hit.astype(jnp.bfloat16)
        for k in range(kv_heads):
            part[k * HALVES + half] = jnp.dot(
                one_hot, fresh[k], preferred_element_type=jnp.float32
            ).astype(jnp.bfloat16)

    for g in range(heads):
        at = (g % group) * rows
        stack[g // group, at : at + rows, :] = queries[:, g * hd : (g + 1) * hd]
    for k in range(kv_heads):
        for at in range(0, columns, 128):
            block = stack[k, at : at + 128, :].astype(jnp.float32)
            q_t[k, :, at : at + 128] = block.T.astype(jnp.bfloat16)
    m_all[...] = jnp.full(m_all.shape, EMPTY, jnp.float32)
    l_all[...] = jnp.zeros(l_all.shape, jnp.float32)
    acc_all[...] = jnp.zeros(acc_all.shape, jnp.float32)

    factor = hd**-0.5 * math.log2(math.e)

    def attend(q, block, own):
        k = q // HALVES
        at = q * ctx_count + block
        keys = kv[at, :length, :]
        values = jnp.concatenate(
            [kv[at, length + i : length + i + 128, :] for i in range(0, length, 128)], axis=1
        )
        scores = jnp.dot(keys, q_t[k], preferred_element_type=jnp.float32)
        if own:
            local = lax.broadcasted_iota(jnp.int32, (length, 1), 0)
            pos = (local // run) * page_len + (q % HALVES) * run + local % run
            scores = jnp.where(pos <= rec_tiled[...], scores, HIDDEN)
        m_old = m_all[k]
        m_new = jnp.maximum(m_old, jnp.max(scores, axis=0, keepdims=True))
        alpha = jnp.exp2((m_old - m_new) * factor)
        weights = jnp.exp2((scores - m_new[:1]) * factor)
        l_all[k] = l_all[k] * alpha + jnp.sum(weights, axis=0, keepdims=True)
        acc_all[k] = acc_all[k] * alpha[:1] + jnp.dot(
            values, weights.astype(jnp.bfloat16), preferred_element_type=jnp.float32
        )
        m_all[k] = m_new

    def along(q, block, sem, to):
        ref = kv.at[q // 2 * ctx_count + block, pl.ds(q % 2 * length, length)]
        return pltpu.make_async_remote_copy(
            ref, ref, ctx_send.at[q, sem], ctx_recv.at[q, block], device_id={"ctx": to}, device_id_type=MESH
        )

    for q in range(pieces):
        others = recvbuf[q].at[pl.ds(0, n - 1)]
        pltpu.make_async_copy(others, others, page_recv.at[q]).wait()
        k, _, lanes = piece_of(q)
        own_part = q // 2 * ctx_count + c

        def place(j, _, q=q, lanes=lanes, own_part=own_part):
            at = idx[0, c * pages + j]
            spot = pl.ds(pl.multiple_of(j * run, run), run)
            page = recvbuf[q][at // 2, at % 2] * keep[q // 2 % HALVES, spot, :] + part[q // 2, spot, lanes]
            if q % 2 == 0:
                kv[own_part, spot, :] = page
            else:
                v_rows[spot, :] = page
            return 0

        lax.fori_loop(0, pages, place, 0)
        if q % 2 == 1:
            for i in range(0, length, 128):
                block = v_rows[i : i + 128, :].astype(jnp.float32)
                kv[own_part, length + i : length + i + 128, :] = block.T.astype(jnp.bfloat16)

        @pl.when(c == 0)
        def _(q=q):
            along(q, 0, 1, 3).start()
            along(q, 0, 0, 1).start()

        @pl.when(c == 1)
        def _(q=q):
            if q % 2 == 1:
                along(q, 1, 1, 0).start()
            along(q, 1, 0, 2).start()

        @pl.when(c == 2)
        def _(q=q):
            along(q, 2, 0, 3).start()

        if q % 2 == 0:
            @pl.when(c == 2)
            def _(q=q):
                along(q, 1, 0, 2).wait_recv()
                along(q, 1, 1, 3).start()

            @pl.when(c == 3)
            def _(q=q):
                along(q, 0, 0, 3).wait_recv()
                along(q, 0, 0, 2).start()

            continue

        attend(q // 2, c, True)

        @pl.when(c == 0)
        def _(q=q):
            along(q, 1, 1, 0).wait_recv()
            along(q, 1, 2, 3).start()

        def earlier(t, _, q=q):
            last = c // 3
            block = last * ((3 - t) % 3) + (1 - last) * (c - 1 - t)

            @pl.when((c == 1) | (t > 0))
            def _():
                along(q - 1, block, 0, c).wait_recv()

            along(q, block, 0, c).wait_recv()

            @pl.when((c == 3) & (t == 0))
            def _():
                along(q, 0, 0, 2).start()

            attend(q // 2, block, False)
            return 0

        lax.fori_loop(0, c, earlier, 0)

    for k in range(kv_heads):
        for at in range(0, columns, 128):
            span = slice(at, at + 128)
            stack[k, span, :] = (acc_all[k, :, span] / l_all[k, :1, span]).T.astype(jnp.bfloat16)
    for g in range(heads):
        at = (g % group) * rows
        out[:, g * hd : (g + 1) * hd] = stack[g // group, at : at + rows, :]

    pltpu.make_async_copy(req.at[pl.ds(0, n - 1)], req.at[pl.ds(0, n - 1)], req_send).wait()
    for q in range(pieces):
        most = sendbuf.at[q, pl.ds(0, n - 1)]
        pltpu.make_async_copy(most, most, page_send.at[q]).wait()

        @pl.when(c == 0)
        def _(q=q):
            along(q, 0, 0, 1).wait_send()
            along(q, 0, 1, 3).wait_send()
            if q % 2 == 1:
                along(q, 1, 2, 3).wait_send()

        @pl.when(c == 1)
        def _(q=q):
            along(q, 1, 0, 2).wait_send()
            if q % 2 == 1:
                along(q, 1, 1, 0).wait_send()

        @pl.when(c == 2)
        def _(q=q):
            along(q, 2, 0, 3).wait_send()
            if q % 2 == 0:
                along(q, 1, 1, 3).wait_send()

        @pl.when(c == 3)
        def _(q=q):
            along(q, 0, 0, 2).wait_send()


def shards(queries, fresh_kv, kv_store, page_owner, page_slot, rec_index):
    n, ctx_count = lax.axis_size("cache"), lax.axis_size("ctx")
    rows, kv_heads, hd = queries.shape[1], fresh_kv.shape[2], fresh_kv.shape[3] // 2
    heads = queries.shape[2] // hd
    slots, page_len = kv_store.shape[:2]
    pages_all = page_owner.shape[1]
    pages = pages_all // ctx_count
    parts, run = kv_heads * HALVES, page_len // HALVES
    pieces, length = 2 * parts, pages * run
    columns = heads // kv_heads * rows
    dims = (n, ctx_count, kv_heads, slots, pages, page_len, rows, heads, hd)
    bf16, f32, i32 = jnp.bfloat16, jnp.float32, jnp.int32
    vmem, anywhere = pl.BlockSpec(memory_space=pltpu.VMEM), pl.BlockSpec(memory_space=pl.ANY)
    dma = pltpu.SemaphoreType.DMA
    result = pl.pallas_call(
        functools.partial(kernel, dims),
        out_shape=jax.ShapeDtypeStruct((rows, heads * hd), bf16),
        in_specs=[vmem, vmem, vmem, anywhere, anywhere, anywhere],
        out_specs=vmem,
        scratch_shapes=[
            pltpu.VMEM((n, 1, 128), i32),
            pltpu.VMEM((n, 1, 128), i32),
            pltpu.SMEM((n, 1, 128), i32),
            pltpu.VMEM((8, pages_all), i32),
            pltpu.SMEM((8, pages_all), i32),
            pltpu.VMEM((slots, page_len, kv_heads, 2 * hd), bf16),
            pltpu.VMEM((rows, kv_heads, 2 * hd), bf16),
            pltpu.VMEM((rows, heads * hd), bf16),
            pltpu.VMEM((slots * kv_heads, page_len, 2 * hd), bf16),
            pltpu.VMEM((pieces, n, 2, run, hd), bf16),
            pltpu.VMEM((parts * ctx_count, 2 * length, hd), bf16),
            pltpu.VMEM((length, hd), bf16),
            pltpu.VMEM((1, columns), i32),
            pltpu.VMEM((kv_heads, rows, 2 * hd), bf16),
            pltpu.VMEM((parts, length, 2 * hd), bf16),
            pltpu.VMEM((HALVES, length, hd), bf16),
            pltpu.VMEM((kv_heads, columns, hd), bf16),
            pltpu.VMEM((kv_heads, hd, columns), bf16),
            pltpu.VMEM((kv_heads, 8, columns), f32),
            pltpu.VMEM((kv_heads, 8, columns), f32),
            pltpu.VMEM((kv_heads, hd, columns), f32),
            dma((3,)), dma, dma, dma((2,)),
            dma((pieces,)), dma((pieces,)),
            dma((pieces, 3)), dma((pieces, ctx_count)),
            *[pltpu.VMEM((n, 2, run, hd), bf16) for _ in range(pieces)],
        ],
        compiler_params=pltpu.CompilerParams(
            collective_id=0, has_side_effects=True, vmem_limit_bytes=48 * 1024 * 1024
        ),
    )(page_owner[0], page_slot, rec_index, kv_store, fresh_kv[0], queries[0])
    return result[None]


def solution(mesh):
    in_specs = (
        P("cache", "ctx", "head"),
        P("cache", "ctx", "head", None),
        P("cache", None, "head", None),
        P("cache", None, None),
        P("cache", None),
        P("cache", None),
    )
    out_specs = P("cache", "ctx", "head")
    return jax.shard_map(shards, mesh=mesh, in_specs=in_specs, out_specs=out_specs, check_vma=False)
```

time: 88.2 us -> 83.3 us (0.944)
  Pallas kernels: 80 us -> 76.2 us
  other arithmetic: 1.78 us -> 0 us
  local copies, waits for them, and re-layouts: 5.54 us -> 6.63 us
    pallas_call x1, Pallas kernels: 80 us -> 76.2 us  [shards(): pl.pallas_call(functools.partial(kernel, dims), out_shape=jax.ShapeDtypeS...]
    unnamed x6 -> x11, local copies, waits for them, and re-layouts: 2.52 us -> 5.87 us
    transpose x1 -> x0, local copies, waits for them, and re-layouts: 2.13 us -> none  [shards(): store = kv_store.transpose(0, 2, 1, 3).reshape(slots * pieces, run, 2 * hd)]
where the time goes in v3:
time: 83.3 us; the launch traced here: 82.8 us
  Pallas kernels  76.2 us (91%)
  local copies, waits for them, and re-layouts  6.63 us (8%)
    pallas_call x1, Pallas kernels, shards(): pl.pallas_call(functools.partial(kernel, dims), out_shape=jax.ShapeDtypeS...  76.2 us
    unnamed x11, local copies, waits for them, and re-layouts  5.87 us

profile of v3, /device:TPU:24, one launch (start us, length us, event | category | flops | bytes accessed | tf_op | source)
XLA Modules:
  0.0 82.8 jit_solution(6211952192298031783)
XLA Ops:
  0.0 0.8 copy.7.owner_col
  0.8 0.0 copy-start
  0.8 1.6 %copy-done = bf16[64,32,2,256]{3,2,1,0:T(2,128)(2,1)S(1)} copy-done((bf16[64,32,2,256]{3,2,1,0:T(2,128)(2,1)S(1)}, bf16[64,32,2,256]{3,2,1,0:T(2,128)(2,1)}, u32[]{:S(2)}) %copy-start) | copy-done | bytes 2097176
  2.4 0.0 copy-start.1
  2.4 1.1 %copy-done.1 = bf16[1,192,2048]{2,1,0:T(8,128)(2,1)S(1)} copy-done((bf16[1,192,2048]{2,1,0:T(8,128)(2,1)S(1)}, bf16[1,192,2048]{2,1,0:T(8,128)(2,1)}, u32[]{:S(2)}) %copy-start.1) | copy-done | bytes 786456
  3.5 0.0 copy-start.2
  3.5 0.9 %copy-done.2 = bf16[1,192,2,256]{3,2,1,0:T(2,128)(2,1)S(1)} copy-done((bf16[1,192,2,256]{3,2,1,0:T(2,128)(2,1)S(1)}, bf16[1,192,2,256]{3,2,1,0:T(2,128)(2,1)}, u32[]{:S(2)}) %copy-start.2) | copy-done | bytes 196632
  4.4 0.0 copy-start.3
  4.4 0.7 copy-done.3
  5.1 0.0 copy-start.4
  5.1 0.7 copy-done.4
  5.8 76.2 %shard_map.64 = bf16[192,2048]{1,0:T(8,128)(2,1)S(1)} custom-call(s32[128,1]{1,0:T(8,128)S(1)} %copy.7.owner_col, s32[1,128]{1,0:T(1,128)S(1)} %copy-done.4, s32[1,768]{1,0:T(1,128)S(1)} %copy-done.3, bf16[64,32,2,256]{3,2,1,0:T(2,128)(2,1)S(1)} %copy-done, bf16[192,2,256]{2,1,0:T(2,128)(2,1)S(1)} %bitcast.6, bf16[192,2048]{1,0:T(8,128)(2,1)S(1)} %bitcast.5), custom_call_target="tpu_custom_call" | custom-call | tf_op jit(solution)/shard_map/pallas_call | solution.py:314
  82.0 0.9 %copy.9 = bf16[1,192,2048]{2,1,0:T(8,128)(2,1)} copy(bf16[1,192,2048]{2,1,0:T(8,128)(2,1)S(1)} %bitcast.4) | data formatting | bytes 1572864
Async XLA Ops:
  0.8 1.6 %copy-start = (bf16[64,32,2,256]{3,2,1,0:T(2,128)(2,1)S(1)}, bf16[64,32,2,256]{3,2,1,0:T(2,128)(2,1)}, u32[]{:S(2)}) copy-start(bf16[64,32,2,256]{3,2,1,0:T(2,128)(2,1)} %raw_in.1) | copy-start | bytes 6291460
  2.4 1.1 %copy-start.1 = (bf16[1,192,2048]{2,1,0:T(8,128)(2,1)S(1)}, bf16[1,192,2048]{2,1,0:T(8,128)(2,1)}, u32[]{:S(2)}) copy-start(bf16[1,192,2048]{2,1,0:T(8,128)(2,1)} %param.6) | copy-start | bytes 2359300
  3.5 0.9 %copy-start.2 = (bf16[1,192,2,256]{3,2,1,0:T(2,128)(2,1)S(1)}, bf16[1,192,2,256]{3,2,1,0:T(2,128)(2,1)}, u32[]{:S(2)}) copy-start(bf16[1,192,2,256]{3,2,1,0:T(2,128)(2,1)} %param.7) | copy-start | bytes 589828
  4.4 0.7 copy-start.3
  5.1 0.7 copy-start.4

commit v4 on v3

--- a/solution.py
+++ b/solution.py
@@ -15,8 +15,8 @@
 
 
 def kernel(
-    dims, owner_col, slot_row, rec_in, raw_in, fresh_in, queries_in, out,
-    req, req_in, req_smem, idx_rows, idx, raw, fresh_raw, queries, store, sendbuf, kv, v_rows, rec_tiled,
+    dims, owner_in, slot_in, rec_hbm, raw_in, fresh_in, queries_in, out,
+    owner_row, slot_row, rec_in, req, req_in, req_smem, idx_rows, idx, raw, fresh_raw, queries, store, sendbuf, kv, v_rows, rec_tiled,
     fresh, part, keep, stack, q_t, m_all, l_all, acc_all,
     load_sem, req_send, req_recv, smem_sem, page_send, page_recv, ctx_send, ctx_recv, *recvbuf,
 ):
@@ -32,6 +32,14 @@
     me = lax.axis_index("cache")
     c = lax.axis_index("ctx")
 
+    arrays = (
+        (owner_in, owner_row), (slot_in, slot_row), (raw_in, raw),
+        (rec_hbm, rec_in), (fresh_in, fresh_raw), (queries_in, queries),
+    )
+    loads = [pltpu.make_async_copy(src, dst, load_sem.at[i]) for i, (src, dst) in enumerate(arrays)]
+    for load in loads:
+        load.start()
+
     barrier = pltpu.get_barrier_semaphore()
 
     def greet(k, _):
@@ -42,27 +50,23 @@
     for step in (1, ctx_count - 1):
         pl.semaphore_signal(barrier, inc=1, device_id={"ctx": lax.rem(c + step, ctx_count)}, device_id_type=MESH)
 
-    loads = [
-        pltpu.make_async_copy(src, dst, load_sem.at[i])
-        for i, (src, dst) in enumerate(((raw_in, raw), (fresh_in, fresh_raw), (queries_in, queries)))
-    ]
-    for load in loads:
-        load.start()
-
     a = lax.broadcasted_iota(i32, (pages_all, pages_all), 0)
     b = lax.broadcasted_iota(i32, (pages_all, pages_all), 1)
-    owner_of_a = jnp.broadcast_to(owner_col[...], (pages_all, pages_all))
-    owner_row = jnp.sum(jnp.where(a == b, owner_of_a, 0), axis=0, keepdims=True)
+    loads[0].wait()
+    loads[1].wait()
+    owner = owner_row[...]
+    owner_f = jnp.broadcast_to(owner, (pages_all, pages_all)).astype(jnp.float32)
+    owner_of_a = jnp.sum(jnp.where(a == b, owner_f, 0.0), axis=1, keepdims=True).astype(i32)
     low = c * pages
-    before = (owner_of_a == owner_row) & (a < b) & (a >= low)
+    before = (owner_of_a == owner) & (a < b) & (a >= low)
     second = jnp.max(jnp.where(before, 1, 0), axis=0, keepdims=True)
-    idx_rows[...] = jnp.broadcast_to(owner_row * 2 + second, idx_rows.shape)
+    idx_rows[...] = jnp.broadcast_to(owner * 2 + second, idx_rows.shape)
     to_idx = pltpu.make_async_copy(idx_rows, idx, smem_sem.at[0])
     to_idx.start()
 
     shard = lax.broadcasted_iota(i32, (n, pages_all), 0)
     place_of = lax.broadcasted_iota(i32, (n, pages_all), 1)
-    named = (shard == owner_row) & (place_of >= low) & (place_of < low + pages)
+    named = (shard == owner) & (place_of >= low) & (place_of < low + pages)
     coded = (place_of * slots + slot_row[...]).astype(jnp.float32)
     first = jnp.min(jnp.where(named, coded, float(pages_all * slots)), axis=1, keepdims=True)
     final = jnp.max(jnp.where(named, coded, 0.0), axis=1, keepdims=True)
@@ -70,7 +74,7 @@
     for d in range(n):
         req[d] = asked[d : d + 1, :]
 
-    loads[0].wait()
+    loads[2].wait()
 
     def split(p, _):
         store[pl.ds(p * kv_heads, kv_heads)] = jnp.swapaxes(raw[p], 0, 1)
@@ -120,17 +124,18 @@
         for r in range(2):
             recvbuf[q][me, r] = page(me, r)
 
+    loads[3].wait()
     fresh_pos = jnp.zeros((1, rows), i32)
     for other in range(ctx_count):
         theirs = rec_in[:, other * rows : (other + 1) * rows]
         fresh_pos = jnp.where(c == other, theirs, fresh_pos)
     for g in range(group):
         rec_tiled[:, g * rows : (g + 1) * rows] = fresh_pos
-    loads[1].wait()
+    loads[4].wait()
     by_head = jnp.swapaxes(fresh_raw[...], 0, 1)
     for k in range(kv_heads):
         fresh[k] = by_head[k]
-    loads[2].wait()
+    loads[5].wait()
     for half in range(HALVES):
         local = lax.broadcasted_iota(jnp.int32, (length, rows), 0)
         pos = (local // run) * page_len + half * run + local % run
@@ -309,14 +314,17 @@
     columns = heads // kv_heads * rows
     dims = (n, ctx_count, kv_heads, slots, pages, page_len, rows, heads, hd)
     bf16, f32, i32 = jnp.bfloat16, jnp.float32, jnp.int32
-    vmem, anywhere = pl.BlockSpec(memory_space=pltpu.VMEM), pl.BlockSpec(memory_space=pl.ANY)
+    vmem, hbm = pl.BlockSpec(memory_space=pltpu.VMEM), pl.BlockSpec(memory_space=pltpu.HBM)
     dma = pltpu.SemaphoreType.DMA
     result = pl.pallas_call(
         functools.partial(kernel, dims),
         out_shape=jax.ShapeDtypeStruct((rows, heads * hd), bf16),
-        in_specs=[vmem, vmem, vmem, anywhere, anywhere, anywhere],
+        in_specs=[hbm] * 6,
         out_specs=vmem,
         scratch_shapes=[
+            pltpu.VMEM((1, pages_all), i32),
+            pltpu.VMEM((1, pages_all), i32),
+            pltpu.VMEM(rec_index.shape, i32),
             pltpu.VMEM((n, 1, 128), i32),
             pltpu.VMEM((n, 1, 128), i32),
             pltpu.SMEM((n, 1, 128), i32),
@@ -338,15 +346,15 @@
             pltpu.VMEM((kv_heads, 8, columns), f32),
             pltpu.VMEM((kv_heads, 8, columns), f32),
             pltpu.VMEM((kv_heads, hd, columns), f32),
-            dma((3,)), dma, dma, dma((2,)),
+            dma((6,)), dma, dma, dma((2,)),
             dma((pieces,)), dma((pieces,)),
             dma((pieces, 3)), dma((pieces, ctx_count)),
             *[pltpu.VMEM((n, 2, run, hd), bf16) for _ in range(pieces)],
         ],
         compiler_params=pltpu.CompilerParams(
-            collective_id=0, has_side_effects=True, vmem_limit_bytes=48 * 1024 * 1024
+            collective_id=0, has_side_effects=True, vmem_limit_bytes=60 * 1024 * 1024
         ),
-    )(page_owner[0], page_slot, rec_index, kv_store, fresh_kv[0], queries[0])
+    )(page_owner[:, :, 0], page_slot, rec_index, kv_store, fresh_kv[0], queries[0])
     return result[None]
 
 

time: 83.3 us -> 79.7 us (0.957)
  local copies, waits for them, and re-layouts: 6.63 us -> 2.09 us
  Pallas kernels: 76.2 us -> 77.3 us
    unnamed x11 -> x1, local copies, waits for them, and re-layouts: 5.87 us -> 2.09 us
    pallas_call x1, Pallas kernels: 76.2 us -> 77.3 us  [shards(): pl.pallas_call(functools.partial(kernel, dims), out_shape=jax.ShapeDtypeS...]
where the time goes in v4:
time: 79.7 us; the launch traced here: 79.4 us
  Pallas kernels  77.3 us (97%)
  local copies, waits for them, and re-layouts  2.09 us (3%)
    pallas_call x1, Pallas kernels, shards(): pl.pallas_call(functools.partial(kernel, dims), out_shape=jax.ShapeDtypeS...  77.3 us
    unnamed x1, local copies, waits for them, and re-layouts  2.09 us

profile of v4, /device:TPU:24, one launch (start us, length us, event | category | flops | bytes accessed | tf_op | source)
XLA Modules:
  0.0 79.4 jit_solution(7257140111441695407)
XLA Ops:
  0.0 77.3 %shard_map.64 = bf16[192,2048]{1,0:T(8,128)(2,1)} custom-call(s32[1,128]{1,0:T(1,128)} %bitcast.7, s32[1,128]{1,0:T(1,128)} %slot_in.1, s32[1,768]{1,0:T(1,128)} %rec_hbm.1, bf16[64,32,2,256]{3,2,1,0:T(2,128)(2,1)} %raw_in.1, bf16[192,2,256]{2,1,0:T(2,128)(2,1)} %bitcast.6, bf16[192,2048]{1,0:T(8,128)(2,1)} %bitcast.5), custom_call_target="tpu_custom_call" | custom-call | tf_op jit(solution)/shard_map/pallas_call | solution.py:319
  77.3 2.1 %copy.8 = bf16[1,192,2048]{2,1,0:T(8,128)(2,1)} copy(bf16[1,192,2048]{2,1,0:T(8,128)(2,1)} %bitcast.4) | data formatting | bytes 1572864

commit v5 on v4

--- a/solution.py
+++ b/solution.py
@@ -12,13 +12,18 @@
 EMPTY = -1e30
 HIDDEN = -2e30
 HALVES = 2
+AHEAD = 3
+LEAD = 2
+PLANE = 4
+SPARE = 2
 
 
 def kernel(
-    dims, owner_in, slot_in, rec_hbm, raw_in, fresh_in, queries_in, out,
+    dims, shared, owner_in, slot_in, rec_hbm, raw_in, fresh_in, queries_in, out, over,
     owner_row, slot_row, rec_in, req, req_in, req_smem, idx_rows, idx, raw, fresh_raw, queries, store, sendbuf, kv, v_rows, rec_tiled,
     fresh, part, keep, stack, q_t, m_all, l_all, acc_all,
-    load_sem, req_send, req_recv, smem_sem, page_send, page_recv, ctx_send, ctx_recv, *recvbuf,
+    load_sem, req_send, req_recv, smem_sem, page_send, page_recv, ctx_send, ctx_recv, hop_send, hop_recv,
+    hop_out, spare_out, *landing,
 ):
     n, ctx_count, kv_heads, slots, pages, page_len, rows, heads, hd = dims
     parts = kv_heads * HALVES
@@ -28,6 +33,8 @@
     group = heads // kv_heads
     columns = group * rows
     pages_all = pages * ctx_count
+    recvbuf, hop_in = landing[:pieces], landing[pieces:]
+    planes = n // PLANE
     i32 = jnp.int32
     me = lax.axis_index("cache")
     c = lax.axis_index("ctx")
@@ -58,9 +65,18 @@
     owner_f = jnp.broadcast_to(owner, (pages_all, pages_all)).astype(jnp.float32)
     owner_of_a = jnp.sum(jnp.where(a == b, owner_f, 0.0), axis=1, keepdims=True).astype(i32)
     low = c * pages
-    before = (owner_of_a == owner) & (a < b) & (a >= low)
-    second = jnp.max(jnp.where(before, 1, 0), axis=0, keepdims=True)
-    idx_rows[...] = jnp.broadcast_to(owner * 2 + second, idx_rows.shape)
+    one_block = a // pages == b // pages
+    alike = (owner_of_a == owner) & one_block
+    second = jnp.max(jnp.where(alike & (a < b), 1, 0), axis=0, keepdims=True)
+    if shared:
+        second_of_a = jnp.max(jnp.where(alike & (b < a), 1.0, 0.0), axis=1, keepdims=True)
+        beside = one_block & (owner_of_a // PLANE == owner // PLANE) & (second_of_a > 0.5)
+        lowest = jnp.min(jnp.where(beside, owner_of_a % PLANE, PLANE), axis=0, keepdims=True)
+        spare = n + owner // PLANE * SPARE + jnp.where(owner % PLANE == lowest, 0, 1)
+        where_to = jnp.where(second > 0, spare, owner)
+    else:
+        where_to = owner * 2 + second
+    idx_rows[...] = jnp.broadcast_to(where_to, idx_rows.shape)
     to_idx = pltpu.make_async_copy(idx_rows, idx, smem_sem.at[0])
     to_idx.start()
 
@@ -71,6 +87,20 @@
     first = jnp.min(jnp.where(named, coded, float(pages_all * slots)), axis=1, keepdims=True)
     final = jnp.max(jnp.where(named, coded, 0.0), axis=1, keepdims=True)
     asked = jnp.where(place_of == 0, first, final).astype(i32) % slots
+    if shared:
+        mine = (shard // PLANE == owner // PLANE) & (second > 0)
+        here = mine & (place_of >= low) & (place_of < low + pages)
+        member = (owner % PLANE).astype(jnp.float32)
+        least = jnp.min(jnp.where(here, member, float(PLANE)), axis=1, keepdims=True).astype(i32) % PLANE
+        most = jnp.max(jnp.where(here, member, 0.0), axis=1, keepdims=True).astype(i32) % PLANE
+        excess = jnp.zeros((n, 1), jnp.float32)
+        for other in range(ctx_count):
+            there = mine & (place_of // pages == other)
+            excess = jnp.maximum(excess, jnp.sum(jnp.where(there, 1.0, 0.0), axis=1, keepdims=True))
+        excess = jnp.max(excess, axis=0, keepdims=True)
+        asked = jnp.where(place_of == 2, least, asked)
+        asked = jnp.where(place_of == 3, most, asked)
+        asked = jnp.where(place_of == 4, jnp.where(excess > SPARE, 1, 0), asked)
     for d in range(n):
         req[d] = asked[d : d + 1, :]
 
@@ -98,31 +128,100 @@
     pltpu.make_async_copy(others, others, req_recv).wait()
     to_smem = pltpu.make_async_copy(req_in, req_smem, smem_sem.at[1])
     to_smem.start()
+    over[...] = jnp.max(req_in[...], axis=0)
     to_smem.wait()
 
     def piece_of(q):
         half, which = q // 2 % HALVES, q % 2
         return q // (2 * HALVES), slice(half * run, (half + 1) * run), slice(which * hd, (which + 1) * hd)
 
-    for q in range(pieces):
+    def page(q, d, r):
         k, span, lanes = piece_of(q)
-
-        def page(d, r, k=k, span=span, lanes=lanes):
-            return store[req_smem[d, 0, r] * kv_heads + k, span, lanes]
-
-        def give(step, _, q=q, page=page):
+        return store[req_smem[d, 0, r] * kv_heads + k, span, lanes]
+
+    z, m = me // PLANE, me % PLANE
+
+    def mate_copy(q, mate):
+        return pltpu.make_async_remote_copy(
+            hop_out.at[q, mate], hop_in[q].at[m], hop_send.at[q], hop_recv.at[q],
+            device_id={"cache": z * PLANE + mate}, device_id_type=MESH,
+        )
+
+    def to_mates(q):
+        def fill(i, _):
+            for mate in range(PLANE):
+                hop_out[q, mate, i] = page(q, i * PLANE + mate, 1)
+            hop_in[q][m, i] = page(q, i * PLANE + m, 1)
+            return 0
+
+        lax.fori_loop(0, planes, fill, 0)
+        for t in range(1, PLANE):
+            mate_copy(q, (m + t) % PLANE).start()
+
+    def give_first(q):
+        def give(step, _):
+            d = lax.rem(me + step, n)
+            sendbuf[q, d, 0] = page(q, d, 0)
+            pltpu.make_async_remote_copy(
+                sendbuf.at[q, d, 0], recvbuf[q].at[me], page_send.at[q], page_recv.at[q],
+                device_id={"cache": d}, device_id_type=MESH,
+            ).start()
+            return 0
+
+        lax.fori_loop(1, n, give, 0)
+        recvbuf[q][me] = page(q, me, 0)
+
+    def give_spare(q):
+        arrived = hop_in[q].at[pl.ds(0, PLANE - 1)]
+        pltpu.make_async_copy(arrived, arrived, hop_recv.at[q]).wait()
+
+        def give(step, _):
+            i = lax.rem(z + step, planes)
+            d = i * PLANE + m
+            for e in range(SPARE):
+                spare_out[q, i, e] = hop_in[q][req_smem[d, 0, 2 + e] & (PLANE - 1), i]
+            pltpu.make_async_remote_copy(
+                spare_out.at[q, i], recvbuf[q].at[pl.ds(n + z * SPARE, SPARE)], page_send.at[q], page_recv.at[q],
+                device_id={"cache": d}, device_id_type=MESH,
+            ).start()
+            return 0
+
+        lax.fori_loop(1, planes, give, 0)
+        for e in range(SPARE):
+            recvbuf[q][n + z * SPARE + e] = hop_in[q][req_smem[me, 0, 2 + e] & (PLANE - 1), z]
+
+    def give_both(q):
+        def give(step, _):
             d = lax.rem(me + step, n)
             for r in range(2):
-                sendbuf[q, d, r] = page(d, r)
+                sendbuf[q, d, r] = page(q, d, r)
             pltpu.make_async_remote_copy(
-                sendbuf.at[q, d], recvbuf[q].at[me], page_send.at[q], page_recv.at[q],
+                sendbuf.at[q, d], recvbuf[q].at[pl.ds(me * 2, 2)], page_send.at[q], page_recv.at[q],
                 device_id={"cache": d}, device_id_type=MESH,
             ).start()
             return 0
 
         lax.fori_loop(1, n, give, 0)
         for r in range(2):
-            recvbuf[q][me, r] = page(me, r)
+            recvbuf[q][me * 2 + r] = page(q, me, r)
+
+    def send(q):
+        if shared:
+            if q < pieces:
+                give_first(q)
+            if q + LEAD < pieces:
+                to_mates(q + LEAD)
+            if 0 < q <= pieces:
+                give_spare(q - 1)
+        elif q < pieces:
+            give_both(q)
+
+    if shared:
+        for q in range(LEAD):
+            to_mates(q)
+    for q in range(AHEAD):
+        send(q)
+    foreign = n - 1 + (planes - 1) * SPARE if shared else 2 * (n - 1)
 
     loads[3].wait()
     fresh_pos = jnp.zeros((1, rows), i32)
@@ -189,8 +288,16 @@
             ref, ref, ctx_send.at[q, sem], ctx_recv.at[q, block], device_id={"ctx": to}, device_id_type=MESH
         )
 
+    def finish(k):
+        for at in range(0, columns, 128):
+            span = slice(at, at + 128)
+            stack[k, span, :] = (acc_all[k, :, span] / l_all[k, :1, span]).T.astype(jnp.bfloat16)
+        for g in range(group):
+            head = k * group + g
+            out[:, head * hd : (head + 1) * hd] = stack[k, g * rows : (g + 1) * rows, :]
+
     for q in range(pieces):
-        others = recvbuf[q].at[pl.ds(0, n - 1)]
+        others = recvbuf[q].at[pl.ds(0, foreign)]
         pltpu.make_async_copy(others, others, page_recv.at[q]).wait()
         k, _, lanes = piece_of(q)
         own_part = q // 2 * ctx_count + c
@@ -198,7 +305,7 @@
         def place(j, _, q=q, lanes=lanes, own_part=own_part):
             at = idx[0, c * pages + j]
             spot = pl.ds(pl.multiple_of(j * run, run), run)
-            page = recvbuf[q][at // 2, at % 2] * keep[q // 2 % HALVES, spot, :] + part[q // 2, spot, lanes]
+            page = recvbuf[q][at] * keep[q // 2 % HALVES, spot, :] + part[q // 2, spot, lanes]
             if q % 2 == 0:
                 kv[own_part, spot, :] = page
             else:
@@ -226,6 +333,8 @@
         def _(q=q):
             along(q, 2, 0, 3).start()
 
+        send(q + AHEAD)
+
         if q % 2 == 0:
             @pl.when(c == 2)
             def _(q=q):
@@ -264,19 +373,16 @@
             return 0
 
         lax.fori_loop(0, c, earlier, 0)
-
-    for k in range(kv_heads):
-        for at in range(0, columns, 128):
-            span = slice(at, at + 128)
-            stack[k, span, :] = (acc_all[k, :, span] / l_all[k, :1, span]).T.astype(jnp.bfloat16)
-    for g in range(heads):
-        at = (g % group) * rows
-        out[:, g * hd : (g + 1) * hd] = stack[g // group, at : at + rows, :]
+        if (q + 1) % (2 * HALVES) == 0:
+            finish(k)
 
     pltpu.make_async_copy(req.at[pl.ds(0, n - 1)], req.at[pl.ds(0, n - 1)], req_send).wait()
     for q in range(pieces):
-        most = sendbuf.at[q, pl.ds(0, n - 1)]
-        pltpu.make_async_copy(most, most, page_send.at[q]).wait()
+        given = recvbuf[q].at[pl.ds(0, foreign)]
+        pltpu.make_async_copy(given, given, page_send.at[q]).wait()
+        if shared:
+            passed = hop_in[q].at[pl.ds(0, PLANE - 1)]
+            pltpu.make_async_copy(passed, passed, hop_send.at[q]).wait()
 
         @pl.when(c == 0)
         def _(q=q):
@@ -316,45 +422,54 @@
     bf16, f32, i32 = jnp.bfloat16, jnp.float32, jnp.int32
     vmem, hbm = pl.BlockSpec(memory_space=pltpu.VMEM), pl.BlockSpec(memory_space=pltpu.HBM)
     dma = pltpu.SemaphoreType.DMA
-    result = pl.pallas_call(
-        functools.partial(kernel, dims),
-        out_shape=jax.ShapeDtypeStruct((rows, heads * hd), bf16),
-        in_specs=[hbm] * 6,
-        out_specs=vmem,
-        scratch_shapes=[
-            pltpu.VMEM((1, pages_all), i32),
-            pltpu.VMEM((1, pages_all), i32),
-            pltpu.VMEM(rec_index.shape, i32),
-            pltpu.VMEM((n, 1, 128), i32),
-            pltpu.VMEM((n, 1, 128), i32),
-            pltpu.SMEM((n, 1, 128), i32),
-            pltpu.VMEM((8, pages_all), i32),
-            pltpu.SMEM((8, pages_all), i32),
-            pltpu.VMEM((slots, page_len, kv_heads, 2 * hd), bf16),
-            pltpu.VMEM((rows, kv_heads, 2 * hd), bf16),
-            pltpu.VMEM((rows, heads * hd), bf16),
-            pltpu.VMEM((slots * kv_heads, page_len, 2 * hd), bf16),
-            pltpu.VMEM((pieces, n, 2, run, hd), bf16),
-            pltpu.VMEM((parts * ctx_count, 2 * length, hd), bf16),
-            pltpu.VMEM((length, hd), bf16),
-            pltpu.VMEM((1, columns), i32),
-            pltpu.VMEM((kv_heads, rows, 2 * hd), bf16),
-            pltpu.VMEM((parts, length, 2 * hd), bf16),
-            pltpu.VMEM((HALVES, length, hd), bf16),
-            pltpu.VMEM((kv_heads, columns, hd), bf16),
-            pltpu.VMEM((kv_heads, hd, columns), bf16),
-            pltpu.VMEM((kv_heads, 8, columns), f32),
-            pltpu.VMEM((kv_heads, 8, columns), f32),
-            pltpu.VMEM((kv_heads, hd, columns), f32),
-            dma((6,)), dma, dma, dma((2,)),
-            dma((pieces,)), dma((pieces,)),
-            dma((pieces, 3)), dma((pieces, ctx_count)),
-            *[pltpu.VMEM((n, 2, run, hd), bf16) for _ in range(pieces)],
-        ],
-        compiler_params=pltpu.CompilerParams(
-            collective_id=0, has_side_effects=True, vmem_limit_bytes=60 * 1024 * 1024
-        ),
-    )(page_owner[:, :, 0], page_slot, rec_index, kv_store, fresh_kv[0], queries[0])
+    def call(shared, *arrays):
+        return pl.pallas_call(
+            functools.partial(kernel, dims, shared),
+            out_shape=[jax.ShapeDtypeStruct((rows, heads * hd), bf16), jax.ShapeDtypeStruct((1, 128), i32)],
+            in_specs=[hbm] * 6,
+            out_specs=[vmem, vmem],
+            scratch_shapes=[
+                pltpu.VMEM((1, pages_all), i32),
+                pltpu.VMEM((1, pages_all), i32),
+                pltpu.VMEM(rec_index.shape, i32),
+                pltpu.VMEM((n, 1, 128), i32),
+                pltpu.VMEM((n, 1, 128), i32),
+                pltpu.SMEM((n, 1, 128), i32),
+                pltpu.VMEM((8, pages_all), i32),
+                pltpu.SMEM((8, pages_all), i32),
+                pltpu.VMEM((slots, page_len, kv_heads, 2 * hd), bf16),
+                pltpu.VMEM((rows, kv_heads, 2 * hd), bf16),
+                pltpu.VMEM((rows, heads * hd), bf16),
+                pltpu.VMEM((slots * kv_heads, page_len, 2 * hd), bf16),
+                pltpu.VMEM((pieces, n, 2, run, hd), bf16),
+                pltpu.VMEM((parts * ctx_count, 2 * length, hd), bf16),
+                pltpu.VMEM((length, hd), bf16),
+                pltpu.VMEM((1, columns), i32),
+                pltpu.VMEM((kv_heads, rows, 2 * hd), bf16),
+                pltpu.VMEM((parts, length, 2 * hd), bf16),
+                pltpu.VMEM((HALVES, length, hd), bf16),
+                pltpu.VMEM((kv_heads, columns, hd), bf16),
+                pltpu.VMEM((kv_heads, hd, columns), bf16),
+                pltpu.VMEM((kv_heads, 8, columns), f32),
+                pltpu.VMEM((kv_heads, 8, columns), f32),
+                pltpu.VMEM((kv_heads, hd, columns), f32),
+                dma((6,)), dma, dma, dma((2,)),
+                dma((pieces,)), dma((pieces,)),
+                dma((pieces, 3)), dma((pieces, ctx_count)),
+                dma((pieces,)), dma((pieces,)),
+                pltpu.VMEM((pieces, PLANE, n // PLANE, run, hd), bf16),
+                pltpu.VMEM((pieces, n // PLANE, SPARE, run, hd), bf16),
+                *[pltpu.VMEM((2 * n, run, hd), bf16) for _ in range(pieces)],
+                *[pltpu.VMEM((PLANE, n // PLANE, run, hd), bf16) for _ in range(pieces)],
+            ],
+            compiler_params=pltpu.CompilerParams(
+                collective_id=0 if shared else 1, has_side_effects=True, vmem_limit_bytes=60 * 1024 * 1024
+            ),
+        )(*arrays)
+
+    arrays = (page_owner[:, :, 0], page_slot, rec_index, kv_store, fresh_kv[0], queries[0])
+    result, over = call(True, *arrays)
+    result = lax.cond(over[0, 4] > 0, lambda: call(False, *arrays)[0], lambda: result)
     return result[None]
 
 

time: 79.7 us -> 76.6 us (0.961)
  Pallas kernels: 77.3 us -> 73.6 us
    pallas_call x1, Pallas kernels: 77.3 us -> 73.6 us  [call(): pl.pallas_call(functools.partial(kernel, dims, shared), out_shape=[jax.Sh...]
    slice x0 -> x1, local copies, waits for them, and re-layouts: none -> 1.23 us  [shards(): over[0, 4] > 0]
    unnamed x1 -> x13, local copies, waits for them, and re-layouts: 2.09 us -> 0.91 us
where the time goes in v5:
time: 76.6 us; the launch traced here: 76.5 us
  Pallas kernels  73.6 us (96%)
  local copies, waits for them, and re-layouts  2.14 us (3%)
    pallas_call x1, Pallas kernels, call(): pl.pallas_call(functools.partial(kernel, dims, shared), out_shape=[jax.Sh...  73.6 us

profile of v5, /device:TPU:24, one launch (start us, length us, event | category | flops | bytes accessed | tf_op | source)
XLA Modules:
  0.0 76.5 jit_solution(6426162335208539652)
XLA Ops:
  0.0 0.0 copy-start.3
  0.0 0.0 copy-start.5
  0.0 0.0 copy-start
  0.0 0.0 copy-start.4
  0.0 0.0 copy-start.2
  0.0 0.0 copy-start.1
  0.0 73.6 %shard_map.66 = (bf16[192,2048]{1,0:T(8,128)(2,1)S(1)}, s32[1,128]{1,0:T(1,128)}) custom-call(s32[1,128]{1,0:T(1,128)} %bitcast.12, s32[1,128]{1,0:T(1,128)} %slot_in.1, s32[1,768]{1,0:T(1,128)} %rec_hbm.1, bf16[64,32,2,256]{3,2,1,0:T(2,128)(2,1)} %raw_in.1, bf16[192,2,256]{2,1,0:T(2,128)(2,1)} %bitcast.8, bf16[192,2048]{1,0:T(8,128)(2,1)} %bitcast.6), custom_call_target="tpu_custom_call" | custom-call | tf_op jit(solution)/shard_map/pallas_call | solution.py:426
  73.6 1.2 %slice.3 = s32[1,1]{1,0:T(1,128)} slice(s32[1,128]{1,0:T(1,128)} %get-tuple-element.32), slice={[0:1], [4:5]} | slice | bytes 8 | tf_op jit(solution)/shard_map/slice | solution.py:472
  75.5 0.0 copy-done.3
  75.5 0.0 copy-done.5
  75.5 0.0 copy-done
  75.5 0.0 copy-done.4
  75.5 0.0 copy-done.2
  75.6 0.0 copy-done.1
  75.6 0.9 %copy.13 = bf16[1,192,2048]{2,1,0:T(8,128)(2,1)} copy(bf16[1,192,2048]{2,1,0:T(8,128)(2,1)S(1)} %get-tuple-element.34) | data formatting | bytes 1572864
  (1 shorter events, 0.0 us)
Async XLA Ops:
  0.0 75.5 %copy-start.3 = (s32[1,768]{1,0:T(1,128)S(1)}, s32[1,768]{1,0:T(1,128)}, u32[]{:S(2)}) copy-start(s32[1,768]{1,0:T(1,128)} %rec_hbm.1) | copy-start | bytes 9220
  0.0 75.5 %copy-start.5 = (s32[1,128]{1,0:T(1,128)S(1)}, s32[1,128]{1,0:T(1,128)}, u32[]{:S(2)}) copy-start(s32[1,128]{1,0:T(1,128)} %slot_in.1) | copy-start | bytes 1540
  0.0 75.5 %copy-start = (bf16[64,32,2,256]{3,2,1,0:T(2,128)(2,1)S(1)}, bf16[64,32,2,256]{3,2,1,0:T(2,128)(2,1)}, u32[]{:S(2)}) copy-start(bf16[64,32,2,256]{3,2,1,0:T(2,128)(2,1)} %raw_in.1) | copy-start | bytes 6291460
  0.0 75.5 %copy-start.4 = (s32[1,128,1]{1,2,0:T(1,128)S(1)}, s32[1,128,1]{1,2,0:T(1,128)}, u32[]{:S(2)}) copy-start(s32[1,128,1]{1,2,0:T(1,128)} %param.11) | copy-start | bytes 1540
  0.0 75.5 %copy-start.2 = (bf16[1,192,2,256]{3,2,1,0:T(2,128)(2,1)S(1)}, bf16[1,192,2,256]{3,2,1,0:T(2,128)(2,1)}, u32[]{:S(2)}) copy-start(bf16[1,192,2,256]{3,2,1,0:T(2,128)(2,1)} %param.9) | copy-start | bytes 589828
  0.0 75.5 %copy-start.1 = (bf16[1,192,2048]{2,1,0:T(8,128)(2,1)S(1)}, bf16[1,192,2048]{2,1,0:T(8,128)(2,1)}, u32[]{:S(2)}) copy-start(bf16[1,192,2048]{2,1,0:T(8,128)(2,1)} %param.8) | copy-start | bytes 2359300

commit v6 on v5

--- a/solution.py
+++ b/solution.py
@@ -296,6 +296,46 @@
             head = k * group + g
             out[:, head * hd : (head + 1) * hd] = stack[k, g * rows : (g + 1) * rows, :]
 
+    def forward(q):
+        if q % 2 == 0:
+
+            @pl.when(c == 2)
+            def _():
+                along(q, 1, 0, 2).wait_recv()
+                along(q, 1, 1, 3).start()
+
+        else:
+
+            @pl.when(c == 0)
+            def _():
+                along(q, 1, 1, 0).wait_recv()
+                along(q, 1, 2, 3).start()
+
+        @pl.when(c == 3)
+        def _():
+            along(q, 0, 0, 3).wait_recv()
+            along(q, 0, 0, 2).start()
+
+    def fold_earlier(p):
+        def earlier(t, _):
+            last = c // 3
+            block = last * ((3 - t) % 3) + (1 - last) * (c - 1 - t)
+
+            @pl.when((c == 1) | (t > 0))
+            def _():
+                along(2 * p, block, 0, c).wait_recv()
+
+            @pl.when((c < 3) | (t > 0))
+            def _():
+                along(2 * p + 1, block, 0, c).wait_recv()
+
+            attend(p, block, False)
+            return 0
+
+        lax.fori_loop(0, c, earlier, 0)
+        if (p + 1) % HALVES == 0:
+            finish(p // HALVES)
+
     for q in range(pieces):
         others = recvbuf[q].at[pl.ds(0, foreign)]
         pltpu.make_async_copy(others, others, page_recv.at[q]).wait()
@@ -335,46 +375,16 @@
 
         send(q + AHEAD)
 
-        if q % 2 == 0:
-            @pl.when(c == 2)
-            def _(q=q):
-                along(q, 1, 0, 2).wait_recv()
-                along(q, 1, 1, 3).start()
-
-            @pl.when(c == 3)
-            def _(q=q):
-                along(q, 0, 0, 3).wait_recv()
-                along(q, 0, 0, 2).start()
-
-            continue
-
-        attend(q // 2, c, True)
-
-        @pl.when(c == 0)
-        def _(q=q):
-            along(q, 1, 1, 0).wait_recv()
-            along(q, 1, 2, 3).start()
-
-        def earlier(t, _, q=q):
-            last = c // 3
-            block = last * ((3 - t) % 3) + (1 - last) * (c - 1 - t)
-
-            @pl.when((c == 1) | (t > 0))
-            def _():
-                along(q - 1, block, 0, c).wait_recv()
-
-            along(q, block, 0, c).wait_recv()
-
-            @pl.when((c == 3) & (t == 0))
-            def _():
-                along(q, 0, 0, 2).start()
-
-            attend(q // 2, block, False)
-            return 0
-
-        lax.fori_loop(0, c, earlier, 0)
-        if (q + 1) % (2 * HALVES) == 0:
-            finish(k)
+        if 0 < q < pieces - 1:
+            forward(q - 1)
+        if q % 2 == 1:
+            attend(q // 2, c, True)
+        elif q > 0:
+            fold_earlier(q // 2 - 1)
+        if q == pieces - 2:
+            forward(q)
+    forward(pieces - 1)
+    fold_earlier(parts - 1)
 
     pltpu.make_async_copy(req.at[pl.ds(0, n - 1)], req.at[pl.ds(0, n - 1)], req_send).wait()
     for q in range(pieces):

time: 76.6 us -> 73.4 us (0.958); the launches traced: 76.5 us -> 72.4 us
  Pallas kernels: 73.6 us -> 69.6 us
    pallas_call x1, Pallas kernels: 73.6 us -> 69.6 us  [call(): pl.pallas_call(functools.partial(kernel, dims, shared), out_shape=[jax.Sh...]
where the time goes in v6:
time: 73.4 us; the launch traced here: 72.4 us
  Pallas kernels  69.6 us (95%)
  local copies, waits for them, and re-layouts  2.14 us (3%)
  between operations  0.75 us (1%)
    pallas_call x1, Pallas kernels, call(): pl.pallas_call(functools.partial(kernel, dims, shared), out_shape=[jax.Sh...  69.6 us

profile of v6, /device:TPU:24, one launch (start us, length us, event | category | flops | bytes accessed | tf_op | source)
XLA Modules:
  0.0 72.4 jit_solution(7378581287832045986)
XLA Ops:
  0.0 0.0 copy-start.3
  0.0 0.0 copy-start.5
  0.0 0.0 copy-start
  0.0 0.0 copy-start.4
  0.0 0.0 copy-start.2
  0.0 0.0 copy-start.1
  0.0 69.6 %shard_map.66 = (bf16[192,2048]{1,0:T(8,128)(2,1)S(1)}, s32[1,128]{1,0:T(1,128)}) custom-call(s32[1,128]{1,0:T(1,128)} %bitcast.12, s32[1,128]{1,0:T(1,128)} %slot_in.1, s32[1,768]{1,0:T(1,128)} %rec_hbm.1, bf16[64,32,2,256]{3,2,1,0:T(2,128)(2,1)} %raw_in.1, bf16[192,2,256]{2,1,0:T(2,128)(2,1)} %bitcast.8, bf16[192,2048]{1,0:T(8,128)(2,1)} %bitcast.6), custom_call_target="tpu_custom_call" | custom-call | tf_op jit(solution)/shard_map/pallas_call | solution.py:436
  69.6 1.2 %slice.3 = s32[1,1]{1,0:T(1,128)} slice(s32[1,128]{1,0:T(1,128)} %get-tuple-element.32), slice={[0:1], [4:5]} | slice | bytes 8 | tf_op jit(solution)/shard_map/slice | solution.py:482
  71.5 0.0 copy-done.3
  71.5 0.0 copy-done.5
  71.5 0.0 copy-done
  71.5 0.0 copy-done.4
  71.5 0.0 copy-done.2
  71.5 0.0 copy-done.1
  71.6 0.9 %copy.13 = bf16[1,192,2048]{2,1,0:T(8,128)(2,1)} copy(bf16[1,192,2048]{2,1,0:T(8,128)(2,1)S(1)} %get-tuple-element.34) | data formatting | bytes 1572864
  (1 shorter events, 0.0 us)
Async XLA Ops:
  0.0 71.5 %copy-start.3 = (s32[1,768]{1,0:T(1,128)S(1)}, s32[1,768]{1,0:T(1,128)}, u32[]{:S(2)}) copy-start(s32[1,768]{1,0:T(1,128)} %rec_hbm.1) | copy-start | bytes 9220
  0.0 71.5 %copy-start.5 = (s32[1,128]{1,0:T(1,128)S(1)}, s32[1,128]{1,0:T(1,128)}, u32[]{:S(2)}) copy-start(s32[1,128]{1,0:T(1,128)} %slot_in.1) | copy-start | bytes 1540
  0.0 71.5 %copy-start = (bf16[64,32,2,256]{3,2,1,0:T(2,128)(2,1)S(1)}, bf16[64,32,2,256]{3,2,1,0:T(2,128)(2,1)}, u32[]{:S(2)}) copy-start(bf16[64,32,2,256]{3,2,1,0:T(2,128)(2,1)} %raw_in.1) | copy-start | bytes 6291460
  0.0 71.5 %copy-start.4 = (s32[1,128,1]{1,2,0:T(1,128)S(1)}, s32[1,128,1]{1,2,0:T(1,128)}, u32[]{:S(2)}) copy-start(s32[1,128,1]{1,2,0:T(1,128)} %param.11) | copy-start | bytes 1540
  0.0 71.5 %copy-start.2 = (bf16[1,192,2,256]{3,2,1,0:T(2,128)(2,1)S(1)}, bf16[1,192,2,256]{3,2,1,0:T(2,128)(2,1)}, u32[]{:S(2)}) copy-start(bf16[1,192,2,256]{3,2,1,0:T(2,128)(2,1)} %param.9) | copy-start | bytes 589828
  0.0 71.5 %copy-start.1 = (bf16[1,192,2048]{2,1,0:T(8,128)(2,1)S(1)}, bf16[1,192,2048]{2,1,0:T(8,128)(2,1)}, u32[]{:S(2)}) copy-start(bf16[1,192,2048]{2,1,0:T(8,128)(2,1)} %param.8) | copy-start | bytes 2359300

commit v7 on v6

--- a/solution.py
+++ b/solution.py
@@ -100,7 +100,7 @@
         excess = jnp.max(excess, axis=0, keepdims=True)
         asked = jnp.where(place_of == 2, least, asked)
         asked = jnp.where(place_of == 3, most, asked)
-        asked = jnp.where(place_of == 4, jnp.where(excess > SPARE, 1, 0), asked)
+        asked = jnp.where(place_of >= 4, jnp.where(excess > SPARE, 1, 0), asked)
     for d in range(n):
         req[d] = asked[d : d + 1, :]
 
@@ -128,7 +128,8 @@
     pltpu.make_async_copy(others, others, req_recv).wait()
     to_smem = pltpu.make_async_copy(req_in, req_smem, smem_sem.at[1])
     to_smem.start()
-    over[...] = jnp.max(req_in[...], axis=0)
+    flags = jnp.max(req_in[...], axis=0).astype(jnp.float32)
+    over[...] = jnp.max(flags[:, 4:], axis=1, keepdims=True).astype(i32)
     to_smem.wait()
 
     def piece_of(q):
@@ -435,7 +436,7 @@
     def call(shared, *arrays):
         return pl.pallas_call(
             functools.partial(kernel, dims, shared),
-            out_shape=[jax.ShapeDtypeStruct((rows, heads * hd), bf16), jax.ShapeDtypeStruct((1, 128), i32)],
+            out_shape=[jax.ShapeDtypeStruct((rows, heads * hd), bf16), jax.ShapeDtypeStruct((1, 1), i32)],
             in_specs=[hbm] * 6,
             out_specs=[vmem, vmem],
             scratch_shapes=[
@@ -479,7 +480,7 @@
 
     arrays = (page_owner[:, :, 0], page_slot, rec_index, kv_store, fresh_kv[0], queries[0])
     result, over = call(True, *arrays)
-    result = lax.cond(over[0, 4] > 0, lambda: call(False, *arrays)[0], lambda: result)
+    result = lax.cond(over[0, 0] > 0, lambda: call(False, *arrays)[0], lambda: result)
     return result[None]
 
 

time: 73.4 us -> 72.1 us (0.982)
  local copies, waits for them, and re-layouts: 2.14 us -> 0.91 us
    slice x1 -> x0, local copies, waits for them, and re-layouts: 1.23 us -> none  [shards(): over[0, 4] > 0]
where the time goes in v7:
time: 72.1 us; the launch traced here: 71.2 us
  Pallas kernels  69.6 us (97%)
  local copies, waits for them, and re-layouts  0.91 us (1%)
    pallas_call x1, Pallas kernels, call(): pl.pallas_call(functools.partial(kernel, dims, shared), out_shape=[jax.Sh...  69.6 us

profile of v7, /device:TPU:24, one launch (start us, length us, event | category | flops | bytes accessed | tf_op | source)
XLA Modules:
  0.0 71.2 jit_solution(11982747914492357543)
XLA Ops:
  0.0 0.0 copy-start.3
  0.0 0.0 copy-start.5
  0.0 0.0 copy-start
  0.0 0.0 copy-start.4
  0.0 0.0 copy-start.2
  0.0 0.0 copy-start.1
  0.0 69.6 %shard_map.66 = (bf16[192,2048]{1,0:T(8,128)(2,1)S(1)}, s32[1,1]{1,0:T(1,128)}) custom-call(s32[1,128]{1,0:T(1,128)} %bitcast.12, s32[1,128]{1,0:T(1,128)} %slot_in.1, s32[1,768]{1,0:T(1,128)} %rec_hbm.1, bf16[64,32,2,256]{3,2,1,0:T(2,128)(2,1)} %raw_in.1, bf16[192,2,256]{2,1,0:T(2,128)(2,1)} %bitcast.8, bf16[192,2048]{1,0:T(8,128)(2,1)} %bitcast.6), custom_call_target="tpu_custom_call" | custom-call | tf_op jit(solution)/shard_map/pallas_call | solution.py:437
  70.2 0.0 copy-done.3
  70.2 0.0 copy-done.5
  70.2 0.0 copy-done
  70.3 0.0 copy-done.4
  70.3 0.0 copy-done.2
  70.3 0.0 copy-done.1
  70.3 0.9 %copy.13 = bf16[1,192,2048]{2,1,0:T(8,128)(2,1)} copy(bf16[1,192,2048]{2,1,0:T(8,128)(2,1)S(1)} %get-tuple-element.34) | data formatting | bytes 1572864
  (1 shorter events, 0.0 us)
Async XLA Ops:
  0.0 70.2 %copy-start.3 = (s32[1,768]{1,0:T(1,128)S(1)}, s32[1,768]{1,0:T(1,128)}, u32[]{:S(2)}) copy-start(s32[1,768]{1,0:T(1,128)} %rec_hbm.1) | copy-start | bytes 9220
  0.0 70.2 %copy-start.5 = (s32[1,128]{1,0:T(1,128)S(1)}, s32[1,128]{1,0:T(1,128)}, u32[]{:S(2)}) copy-start(s32[1,128]{1,0:T(1,128)} %slot_in.1) | copy-start | bytes 1540
  0.0 70.2 %copy-start = (bf16[64,32,2,256]{3,2,1,0:T(2,128)(2,1)S(1)}, bf16[64,32,2,256]{3,2,1,0:T(2,128)(2,1)}, u32[]{:S(2)}) copy-start(bf16[64,32,2,256]{3,2,1,0:T(2,128)(2,1)} %raw_in.1) | copy-start | bytes 6291460
  0.0 70.2 %copy-start.4 = (s32[1,128,1]{1,2,0:T(1,128)S(1)}, s32[1,128,1]{1,2,0:T(1,128)}, u32[]{:S(2)}) copy-start(s32[1,128,1]{1,2,0:T(1,128)} %param.11) | copy-start | bytes 1540
  0.0 70.2 %copy-start.2 = (bf16[1,192,2,256]{3,2,1,0:T(2,128)(2,1)S(1)}, bf16[1,192,2,256]{3,2,1,0:T(2,128)(2,1)}, u32[]{:S(2)}) copy-start(bf16[1,192,2,256]{3,2,1,0:T(2,128)(2,1)} %param.9) | copy-start | bytes 589828
  0.0 70.2 %copy-start.1 = (bf16[1,192,2048]{2,1,0:T(8,128)(2,1)S(1)}, bf16[1,192,2048]{2,1,0:T(8,128)(2,1)}, u32[]{:S(2)}) copy-start(bf16[1,192,2048]{2,1,0:T(8,128)(2,1)} %param.8) | copy-start | bytes 2359300

commit v8 on v7

--- a/solution.py
+++ b/solution.py
@@ -124,106 +124,6 @@
     lax.fori_loop(1, n, ask, 0)
     req_in[me] = req[me]
 
-    others = req_in.at[pl.ds(0, n - 1)]
-    pltpu.make_async_copy(others, others, req_recv).wait()
-    to_smem = pltpu.make_async_copy(req_in, req_smem, smem_sem.at[1])
-    to_smem.start()
-    flags = jnp.max(req_in[...], axis=0).astype(jnp.float32)
-    over[...] = jnp.max(flags[:, 4:], axis=1, keepdims=True).astype(i32)
-    to_smem.wait()
-
-    def piece_of(q):
-        half, which = q // 2 % HALVES, q % 2
-        return q // (2 * HALVES), slice(half * run, (half + 1) * run), slice(which * hd, (which + 1) * hd)
-
-    def page(q, d, r):
-        k, span, lanes = piece_of(q)
-        return store[req_smem[d, 0, r] * kv_heads + k, span, lanes]
-
-    z, m = me // PLANE, me % PLANE
-
-    def mate_copy(q, mate):
-        return pltpu.make_async_remote_copy(
-            hop_out.at[q, mate], hop_in[q].at[m], hop_send.at[q], hop_recv.at[q],
-            device_id={"cache": z * PLANE + mate}, device_id_type=MESH,
-        )
-
-    def to_mates(q):
-        def fill(i, _):
-            for mate in range(PLANE):
-                hop_out[q, mate, i] = page(q, i * PLANE + mate, 1)
-            hop_in[q][m, i] = page(q, i * PLANE + m, 1)
-            return 0
-
-        lax.fori_loop(0, planes, fill, 0)
-        for t in range(1, PLANE):
-            mate_copy(q, (m + t) % PLANE).start()
-
-    def give_first(q):
-        def give(step, _):
-            d = lax.rem(me + step, n)
-            sendbuf[q, d, 0] = page(q, d, 0)
-            pltpu.make_async_remote_copy(
-                sendbuf.at[q, d, 0], recvbuf[q].at[me], page_send.at[q], page_recv.at[q],
-                device_id={"cache": d}, device_id_type=MESH,
-            ).start()
-            return 0
-
-        lax.fori_loop(1, n, give, 0)
-        recvbuf[q][me] = page(q, me, 0)
-
-    def give_spare(q):
-        arrived = hop_in[q].at[pl.ds(0, PLANE - 1)]
-        pltpu.make_async_copy(arrived, arrived, hop_recv.at[q]).wait()
-
-        def give(step, _):
-            i = lax.rem(z + step, planes)
-            d = i * PLANE + m
-            for e in range(SPARE):
-                spare_out[q, i, e] = hop_in[q][req_smem[d, 0, 2 + e] & (PLANE - 1), i]
-            pltpu.make_async_remote_copy(
-                spare_out.at[q, i], recvbuf[q].at[pl.ds(n + z * SPARE, SPARE)], page_send.at[q], page_recv.at[q],
-                device_id={"cache": d}, device_id_type=MESH,
-            ).start()
-            return 0
-
-        lax.fori_loop(1, planes, give, 0)
-        for e in range(SPARE):
-            recvbuf[q][n + z * SPARE + e] = hop_in[q][req_smem[me, 0, 2 + e] & (PLANE - 1), z]
-
-    def give_both(q):
-        def give(step, _):
-            d = lax.rem(me + step, n)
-            for r in range(2):
-                sendbuf[q, d, r] = page(q, d, r)
-            pltpu.make_async_remote_copy(
-                sendbuf.at[q, d], recvbuf[q].at[pl.ds(me * 2, 2)], page_send.at[q], page_recv.at[q],
-                device_id={"cache": d}, device_id_type=MESH,
-            ).start()
-            return 0
-
-        lax.fori_loop(1, n, give, 0)
-        for r in range(2):
-            recvbuf[q][me * 2 + r] = page(q, me, r)
-
-    def send(q):
-        if shared:
-            if q < pieces:
-                give_first(q)
-            if q + LEAD < pieces:
-                to_mates(q + LEAD)
-            if 0 < q <= pieces:
-                give_spare(q - 1)
-        elif q < pieces:
-            give_both(q)
-
-    if shared:
-        for q in range(LEAD):
-            to_mates(q)
-    for q in range(AHEAD):
-        send(q)
-    foreign = n - 1 + (planes - 1) * SPARE if shared else 2 * (n - 1)
-
     loads[3].wait()
     fresh_pos = jnp.zeros((1, rows), i32)
     for other in range(ctx_count):
@@ -235,7 +135,6 @@
     by_head = jnp.swapaxes(fresh_raw[...], 0, 1)
     for k in range(kv_heads):
         fresh[k] = by_head[k]
-    loads[5].wait()
     for half in range(HALVES):
         local = lax.broadcasted_iota(jnp.int32, (length, rows), 0)
         pos = (local // run) * page_len + half * run + local % run
@@ -248,6 +147,107 @@
                 one_hot, fresh[k], preferred_element_type=jnp.float32
             ).astype(jnp.bfloat16)
 
+    others = req_in.at[pl.ds(0, n - 1)]
+    pltpu.make_async_copy(others, others, req_recv).wait()
+    to_smem = pltpu.make_async_copy(req_in, req_smem, smem_sem.at[1])
+    to_smem.start()
+    flags = jnp.max(req_in[...], axis=0).astype(jnp.float32)
+    over[...] = jnp.max(flags[:, 4:], axis=1, keepdims=True).astype(i32)
+    to_smem.wait()
+
+    def piece_of(q):
+        half, which = q // 2 % HALVES, q % 2
+        return q // (2 * HALVES), slice(half * run, (half + 1) * run), slice(which * hd, (which + 1) * hd)
+
+    def page(q, d, r):
+        k, span, lanes = piece_of(q)
+        return store[req_smem[d, 0, r] * kv_heads + k, span, lanes]
+
+    z, m = me // PLANE, me % PLANE
+
+    def mate_copy(q, mate):
+        return pltpu.make_async_remote_copy(
+            hop_out.at[q, mate], hop_in[q].at[m], hop_send.at[q], hop_recv.at[q],
+            device_id={"cache": z * PLANE + mate}, device_id_type=MESH,
+        )
+
+    def to_mates(q):
+        def fill(i, _):
+            for mate in range(PLANE):
+                hop_out[q, mate, i] = page(q, i * PLANE + mate, 1)
+            hop_in[q][m, i] = page(q, i * PLANE + m, 1)
+            return 0
+
+        lax.fori_loop(0, planes, fill, 0)
+        for t in range(1, PLANE):
+            mate_copy(q, (m + t) % PLANE).start()
+
+    def give_first(q):
+        def give(step, _):
+            d = lax.rem(me + step, n)
+            sendbuf[q, d, 0] = page(q, d, 0)
+            pltpu.make_async_remote_copy(
+                sendbuf.at[q, d, 0], recvbuf[q].at[me], page_send.at[q], page_recv.at[q],
+                device_id={"cache": d}, device_id_type=MESH,
+            ).start()
+            return 0
+
+        lax.fori_loop(1, n, give, 0)
+        recvbuf[q][me] = page(q, me, 0)
+
+    def give_spare(q):
+        arrived = hop_in[q].at[pl.ds(0, PLANE - 1)]
+        pltpu.make_async_copy(arrived, arrived, hop_recv.at[q]).wait()
+
+        def give(step, _):
+            i = lax.rem(z + step, planes)
+            d = i * PLANE + m
+            for e in range(SPARE):
+                spare_out[q, i, e] = hop_in[q][req_smem[d, 0, 2 + e] & (PLANE - 1), i]
+            pltpu.make_async_remote_copy(
+                spare_out.at[q, i], recvbuf[q].at[pl.ds(n + z * SPARE, SPARE)], page_send.at[q], page_recv.at[q],
+                device_id={"cache": d}, device_id_type=MESH,
+            ).start()
+            return 0
+
+        lax.fori_loop(1, planes, give, 0)
+        for e in range(SPARE):
+            recvbuf[q][n + z * SPARE + e] = hop_in[q][req_smem[me, 0, 2 + e] & (PLANE - 1), z]
+
+    def give_both(q):
+        def give(step, _):
+            d = lax.rem(me + step, n)
+            for r in range(2):
+                sendbuf[q, d, r] = page(q, d, r)
+            pltpu.make_async_remote_copy(
+                sendbuf.at[q, d], recvbuf[q].at[pl.ds(me * 2, 2)], page_send.at[q], page_recv.at[q],
+                device_id={"cache": d}, device_id_type=MESH,
+            ).start()
+            return 0
+
+        lax.fori_loop(1, n, give, 0)
+        for r in range(2):
+            recvbuf[q][me * 2 + r] = page(q, me, r)
+
+    def send(q):
+        if shared:
+            if q < pieces:
+                give_first(q)
+            if q + LEAD < pieces:
+                to_mates(q + LEAD)
+            if 0 < q <= pieces:
+                give_spare(q - 1)
+        elif q < pieces:
+            give_both(q)
+
+    if shared:
+        for q in range(LEAD):
+            to_mates(q)
+    for q in range(AHEAD):
+        send(q)
+    foreign = n - 1 + (planes - 1) * SPARE if shared else 2 * (n - 1)
+
+    loads[5].wait()
     for g in range(heads):
         at = (g % group) * rows
         stack[g // group, at : at + rows, :] = queries[:, g * hd : (g + 1) * hd]

time: 72.1 us -> 72.1 us (level)
  no operation moved by 1% of the time
where the time goes in v8:
time: 72.1 us; the launch traced here: 71.2 us
  Pallas kernels  69.6 us (97%)
  local copies, waits for them, and re-layouts  0.91 us (1%)
    pallas_call x1, Pallas kernels, call(): pl.pallas_call(functools.partial(kernel, dims, shared), out_shape=[jax.Sh...  69.6 us

profile of v8, /device:TPU:24, one launch (start us, length us, event | category | flops | bytes accessed | tf_op | source)
XLA Modules:
  0.0 71.2 jit_solution(1266047284134346765)
XLA Ops:
  0.0 0.0 copy-start.3
  0.0 0.0 copy-start.5
  0.0 0.0 copy-start
  0.0 0.0 copy-start.4
  0.0 0.0 copy-start.2
  0.0 0.0 copy-start.1
  0.0 69.6 %shard_map.66 = (bf16[192,2048]{1,0:T(8,128)(2,1)S(1)}, s32[1,1]{1,0:T(1,128)}) custom-call(s32[1,128]{1,0:T(1,128)} %bitcast.12, s32[1,128]{1,0:T(1,128)} %slot_in.1, s32[1,768]{1,0:T(1,128)} %rec_hbm.1, bf16[64,32,2,256]{3,2,1,0:T(2,128)(2,1)} %raw_in.1, bf16[192,2,256]{2,1,0:T(2,128)(2,1)} %bitcast.8, bf16[192,2048]{1,0:T(8,128)(2,1)} %bitcast.6), custom_call_target="tpu_custom_call" | custom-call | tf_op jit(solution)/shard_map/pallas_call | solution.py:437
  70.3 0.0 copy-done.3
  70.3 0.0 copy-done.5
  70.3 0.0 copy-done
  70.3 0.0 copy-done.4
  70.3 0.0 copy-done.2
  70.3 0.0 copy-done.1
  70.3 0.9 %copy.13 = bf16[1,192,2048]{2,1,0:T(8,128)(2,1)} copy(bf16[1,192,2048]{2,1,0:T(8,128)(2,1)S(1)} %get-tuple-element.34) | data formatting | bytes 1572864
  (1 shorter events, 0.0 us)
Async XLA Ops:
  0.0 70.3 %copy-start.3 = (s32[1,768]{1,0:T(1,128)S(1)}, s32[1,768]{1,0:T(1,128)}, u32[]{:S(2)}) copy-start(s32[1,768]{1,0:T(1,128)} %rec_hbm.1) | copy-start | bytes 9220
  0.0 70.3 %copy-start.5 = (s32[1,128]{1,0:T(1,128)S(1)}, s32[1,128]{1,0:T(1,128)}, u32[]{:S(2)}) copy-start(s32[1,128]{1,0:T(1,128)} %slot_in.1) | copy-start | bytes 1540
  0.0 70.3 %copy-start = (bf16[64,32,2,256]{3,2,1,0:T(2,128)(2,1)S(1)}, bf16[64,32,2,256]{3,2,1,0:T(2,128)(2,1)}, u32[]{:S(2)}) copy-start(bf16[64,32,2,256]{3,2,1,0:T(2,128)(2,1)} %raw_in.1) | copy-start | bytes 6291460
  0.0 70.3 %copy-start.4 = (s32[1,128,1]{1,2,0:T(1,128)S(1)}, s32[1,128,1]{1,2,0:T(1,128)}, u32[]{:S(2)}) copy-start(s32[1,128,1]{1,2,0:T(1,128)} %param.11) | copy-start | bytes 1540
  0.0 70.3 %copy-start.2 = (bf16[1,192,2,256]{3,2,1,0:T(2,128)(2,1)S(1)}, bf16[1,192,2,256]{3,2,1,0:T(2,128)(2,1)}, u32[]{:S(2)}) copy-start(bf16[1,192,2,256]{3,2,1,0:T(2,128)(2,1)} %param.9) | copy-start | bytes 589828
  0.0 70.3 %copy-start.1 = (bf16[1,192,2048]{2,1,0:T(8,128)(2,1)S(1)}, bf16[1,192,2048]{2,1,0:T(8,128)(2,1)}, u32[]{:S(2)}) copy-start(bf16[1,192,2048]{2,1,0:T(8,128)(2,1)} %param.8) | copy-start | bytes 2359300
